TPU v7x, 512 devices: a whole 4x8x8 slice. The times are simulated.
512 devices in a mesh: dp: 16 (over y_lo, x, core), ctx: 32 (over y_hi, z).
Axes of the slice: x: 4, y: 8 (y_hi: 4, y_lo: 2; y = y_hi * 2 + y_lo), z: 8, core: 2. Of those that a mesh axis runs over, the one named last changes fastest.
Arguments:
- queries: bfloat16 [65536, 512], P(('dp', 'ctx')), may hold values from -16 to 16
- keyvals: bfloat16 [65536, 1024], P(('dp', 'ctx')), may hold values from -4 to 4
- out_weight: bfloat16 [1024, 512], P('ctx'), may hold values from -0.25 to 0.25
- out_grad: bfloat16 [65536, 1024], P(('dp', 'ctx')), may hold values from -24 to 24
- block_lists: int32 [16, 64, 8], P('dp'), may hold values from 0 to 63, as said below
- block_counts: int32 [16, 64], P('dp'), may hold values from 2 to 8, as said below
- seq_lengths: int32 [16], P('dp'), may hold values from 2048 to 4096, as said below
Outputs:
- query_grad: bfloat16 [65536, 512], P(('dp', 'ctx'))
- keyval_grad: bfloat16 [65536, 1024], P(('dp', 'ctx'))
- weight_grad: float32 [1024, 512], P('ctx')
Inputs may be any that keep to these rules, and one draw needn't show every extreme that they name: block_lists[s, b, 0] = b. Entry j >= 1 names a block owned by another index of ctx (owner = block // 2); the owners within one list are distinct, and all entries of the query blocks of one owner of ctx that name the same owner name the same block of it. `block_counts`: some query block of every sequence uses all 8 entries. `seq_lengths`: some sequence is full.
All inputs are finite; a program needn't handle non-finite values.
Results may differ from a plain program's by a relative error of at most 0.025.
Values may be sent and summed in bfloat16 or wider, within the bound.
A program may use at most 128 MiB of HBM per device.

v0:
```python
import math

import jax
import jax.numpy as jnp
from jax import lax
from jax.sharding import PartitionSpec as P

HEADS = 8
HEAD_DIM = 64
BLK = 64
KPQ = 8


def per_device(queries, keyvals, out_weight, out_grad, block_lists, block_counts, seq_lengths):
    ctx_ranks = lax.axis_size("ctx")
    own_rank = lax.axis_index("ctx")
    row_count = queries.shape[0]
    blocks_here = row_count // BLK
    width_two = keyvals.shape[1]
    block_list = block_lists[0]
    counts = block_counts[0]
    length = seq_lengths[0]
    factor = 1.0 / math.sqrt(HEAD_DIM)
    entries = jnp.arange(KPQ, dtype=jnp.int32)
    block_ids = jnp.arange(blocks_here, dtype=jnp.int32)
    rank_ids = jnp.arange(ctx_ranks, dtype=jnp.int32)
    owner_rank = block_list // blocks_here
    needed = (
        (entries[None, :] >= 1) & (entries[None, :] < counts[:, None]) & (owner_rank == own_rank)
    )
    wanted = (
        jnp.where(needed, block_list % blocks_here, 0)
        .reshape(ctx_ranks, blocks_here * KPQ)
        .max(axis=1)
    )
    select_out = (wanted[:, None] == block_ids[None, :]).astype(jnp.bfloat16)
    kv_flat = keyvals.reshape(blocks_here, BLK * width_two)
    outgoing = jnp.dot(select_out, kv_flat, preferred_element_type=jnp.float32).astype(jnp.bfloat16)
    incoming = lax.all_to_all(
        outgoing.reshape(ctx_ranks, BLK, width_two), "ctx", split_axis=0, concat_axis=0, tiled=True
    )
    first_block = own_rank * blocks_here
    mine = lax.dynamic_slice_in_dim(block_list, first_block, blocks_here, 0)
    my_counts = lax.dynamic_slice_in_dim(counts, first_block, blocks_here, 0)
    remote_rank = mine[:, 1:] // blocks_here
    remote_rows = incoming[remote_rank]
    gathered = jnp.concatenate(
        [keyvals.reshape(blocks_here, 1, BLK, width_two), remote_rows], axis=1
    )
    gathered = gathered.reshape(blocks_here, KPQ * BLK, 2, HEADS, HEAD_DIM)
    key_part = gathered[:, :, 0]
    value_part = gathered[:, :, 1]
    query_pos = (first_block * BLK + jnp.arange(row_count, dtype=jnp.int32)).reshape(
        blocks_here, BLK
    )
    valid_rows = query_pos < length
    key_pos = (mine[:, :, None] * BLK + jnp.arange(BLK, dtype=jnp.int32)[None, None, :]).reshape(
        blocks_here, KPQ * BLK
    )
    active = jnp.repeat(entries[None, :] < my_counts[:, None], BLK, axis=1)
    allowed = active[:, None, :] & (
        (key_pos < length)[:, None, :] | (key_pos[:, None, :] == query_pos[:, :, None])
    )
    query = queries.reshape(blocks_here, BLK, HEADS, HEAD_DIM)
    scores = (
        jnp.einsum("bihd,bjhd->bhij", query, key_part, preferred_element_type=jnp.float32) * factor
    )
    scores = jnp.where(allowed[:, None], scores, -jnp.inf)
    row_max = jnp.max(scores, axis=-1, keepdims=True)
    exponent = jnp.exp(scores - row_max)
    prob_bf16 = (exponent / jnp.sum(exponent, axis=-1, keepdims=True)).astype(jnp.bfloat16)
    attended = jnp.einsum(
        "bhij,bjhd->bihd", prob_bf16, value_part, preferred_element_type=jnp.float32
    )
    attention = (attended * valid_rows[:, :, None, None].astype(jnp.float32)).astype(jnp.bfloat16)
    attention_rows = attention.reshape(row_count, HEADS * HEAD_DIM)
    full_weight = lax.all_gather(out_weight, "ctx", axis=0, tiled=True)
    attn_full = jnp.dot(out_grad, full_weight, preferred_element_type=jnp.float32)
    attn_grad = (attn_full * valid_rows.reshape(row_count, 1).astype(jnp.float32)).astype(
        jnp.bfloat16
    )
    grad_heads = attn_grad.reshape(blocks_here, BLK, HEADS, HEAD_DIM)
    row_delta = jnp.sum(grad_heads.astype(jnp.float32) * attention.astype(jnp.float32), axis=-1)
    row_delta = jnp.transpose(row_delta, (0, 2, 1))
    prob_grad = jnp.einsum(
        "bihd,bjhd->bhij", grad_heads, value_part, preferred_element_type=jnp.float32
    )
    score_grad = (prob_bf16.astype(jnp.float32) * (prob_grad - row_delta[..., None])).astype(
        jnp.bfloat16
    )
    query_grad = (
        jnp.einsum("bhij,bjhd->bihd", score_grad, key_part, preferred_element_type=jnp.float32)
        * factor
    )
    query_grad = query_grad.astype(jnp.bfloat16).reshape(row_count, HEADS * HEAD_DIM)
    key_grad = (
        jnp.einsum("bhij,bihd->bjhd", score_grad, query, preferred_element_type=jnp.float32)
        * factor
    )
    value_grad = jnp.einsum(
        "bhij,bihd->bjhd", prob_bf16, grad_heads, preferred_element_type=jnp.float32
    )
    entry_grads = jnp.stack([key_grad, value_grad], axis=2).reshape(
        blocks_here, KPQ, BLK * width_two
    )
    local_part = entry_grads[:, 0]
    remote_terms = entry_grads[:, 1:].reshape(blocks_here * (KPQ - 1), BLK * width_two)
    owner_table = (rank_ids[:, None] == remote_rank.reshape(1, -1)).astype(jnp.float32)
    remote = jnp.dot(
        owner_table,
        remote_terms,
        precision=lax.Precision.HIGHEST,
        preferred_element_type=jnp.float32,
    )
    returned = lax.all_to_all(
        remote.reshape(ctx_ranks, BLK, width_two).astype(jnp.bfloat16),
        "ctx",
        split_axis=0,
        concat_axis=0,
        tiled=True,
    ).astype(jnp.float32)
    back_table = (block_ids[:, None] == wanted[None, :]).astype(jnp.float32)
    added = jnp.dot(
        back_table,
        returned.reshape(ctx_ranks, BLK * width_two),
        precision=lax.Precision.HIGHEST,
        preferred_element_type=jnp.float32,
    )
    keyval_grad = (local_part + added).reshape(row_count, width_two).astype(jnp.bfloat16)
    groups = lax.axis_size("dp")
    scaling = 1.0 / math.sqrt(row_count * ctx_ranks * groups)
    shard_sum = lax.psum_scatter(
        (
            lax.dot_general(
                out_grad,
                attention_rows,
                (((0,), (0,)), ((), ())),
                preferred_element_type=jnp.float32,
            )
            * scaling
        ).astype(jnp.bfloat16),
        "ctx",
        scatter_dimension=0,
        tiled=True,
    )
    weight_grad = lax.psum(shard_sum, "dp").astype(jnp.float32)
    return (query_grad, keyval_grad, weight_grad)


def solution(mesh):
    placed = (
        P(("dp", "ctx"), None),
        P(("dp", "ctx"), None),
        P("ctx", None),
        P(("dp", "ctx"), None),
        P("dp", None, None),
        P("dp", None),
        P("dp"),
    )
    return jax.shard_map(
        per_device,
        mesh=mesh,
        in_specs=placed,
        out_specs=(P(("dp", "ctx"), None), P(("dp", "ctx"), None), P("ctx", None)),
        check_vma=False,
    )
```

profile of v0, /device:TPU:1, one launch (start us, length us, event | category | flops | bytes accessed | tf_op | source)
XLA Modules:
  0.0 642.0 jit_solution(8947203091439883229)
XLA Ops:
  7.2 0.8 fusion.31
  8.1 1.2 reshape.187
  9.4 1.3 convolution_convert_fusion
  10.7 4.3 copy.55
  15.0 16.8 %all-to-all-start = ((bf16[32,64,1024]{2,1,0:T(8,128)(2,1)}), bf16[32,64,1024]{2,1,0:T(8,128)(2,1)}, u32[]{:S(2)}, u32[]{:S(2)}) async-start(bf16[32,64,1024]{2,1,0:T(8,128)(2,1)} %bitcast.97), calls=%async_computation | async-start | bytes 8388608 | tf_op jit(solution)/shard_map/all_to_all | solution.py:39
  31.8 0.7 all-gather.2.cloned.1.call-update
  34.4 0.9 copy.42
  35.4 157.5 %all-gather.2.cloned.1.call-done = bf16[1024,512]{1,0:T(8,128)(2,1)} async-done(((bf16[32,512]{1,0:T(8,128)(2,1)}), bf16[1024,512]{1,0:T(8,128)(2,1)}) %all-gather.2.cloned.1.call-update) | async-done | bytes 1048592 | tf_op jit(solution)/shard_map/all_gather | solution.py:77
  192.9 1.5 fusion.13
  194.7 0.9 copy.40
  195.6 4.1 gather_fusion
  199.8 1.7 pad_maximum_fusion.1
  201.4 4.2 reshape.189
  205.6 3.8 fusion.44
  209.4 3.3 copy.53
  212.7 1.4 copy.52
  214.2 1.8 fusion.45
  216.0 0.2 divide_convert_fusion
  216.2 0.7 copy-done.2
  216.9 0.4 convolution_bitcast_fusion
  217.4 0.8 copy-done.1
  218.2 1.2 multiply_reduce_fusion
  219.3 0.5 multiply_convert_fusion.1
  219.8 0.4 copy-done.4
  220.3 0.4 multiply_bitcast_fusion
  220.7 2.5 pad_maximum_fusion
  223.2 8.1 %copy.44 = f32[2,512,2,8,64]{4,3,2,1,0:T(8,128)} copy(f32[2,512,2,8,64]{1,4,3,0,2:T(8,128)} %pad_maximum_fusion) | data formatting | bytes 8388608 | tf_op jit(solution)/shard_map/stack | solution.py:103
  231.4 6.0 reshape.193
  237.4 4.5 slice.25
  241.8 4.7 reshape.194
  246.5 4.6 copy.56
  251.2 0.5 slice_bitcast_fusion
  251.7 5.8 fusion.4
  257.4 4.3 copy.47
  261.8 7.7 %all-to-all-start.1 = ((bf16[32,64,1024]{2,1,0:T(8,128)(2,1)}), bf16[32,64,1024]{2,1,0:T(8,128)(2,1)}, u32[]{:S(2)}, u32[]{:S(2)}) async-start(bf16[32,64,1024]{2,1,0:T(8,128)(2,1)} %copy.47), calls=%async_computation.1 | async-start | bytes 8388608 | tf_op jit(solution)/shard_map/all_to_all | solution.py:115
  269.5 0.2 copy.48
  269.7 0.2 reshape.196
  269.9 0.5 fusion.8
  270.4 1.3 copy.50
  271.8 0.4 fusion.11
  272.4 0.9 reshape.192
  273.3 299.6 %reduce-scatter.4.cloned.1.call-done = bf16[32,512]{1,0:T(8,128)(2,1)} async-done(((bf16[1024,512]{1,0:T(8,128)(2,1)}), bf16[32,512]{1,0:T(8,128)(2,1)}) %reduce-scatter.4.cloned.1.call-update) | async-done | bytes 32784
  572.9 0.9 copy.51
  573.7 54.4 %psum.7 = bf16[32,512]{0,1:T(8,128)(2,1)S(1)} all-reduce(bf16[32,512]{0,1:T(8,128)(2,1)S(1)} %copy.51), channel_id=1, replica_groups=mesh['dp'=16,'ctx'=32] {'dp'}, use_global_device_ids=true, to_apply=%region_6.7 | all-reduce | flops 16384 | bytes 65536 | tf_op jit(solution)/shard_map/psum | solution.py:146
  628.1 0.7 copy.49
  628.8 4.6 copy.57
  633.4 0.8 fusion.1
  634.2 0.9 convert_element_type.86
  (48 shorter events, 2.0 us)
Async XLA Ops:
  7.2 185.8 %copy-start = (bf16[128,1024]{1,0:T(8,128)(2,1)S(1)}, bf16[128,1024]{1,0:T(8,128)(2,1)}, u32[]{:S(2)}) copy-start(bf16[128,1024]{1,0:T(8,128)(2,1)} %param.10) | copy-start | bytes 786436
  15.0 18.2 %copy-start.8 = (s32[1,64]{1,0:T(1,128)S(1)}, s32[1,64]{1,0:T(1,128)}, u32[]{:S(2)}) copy-start(s32[1,64]{1,0:T(1,128)} %param.12) | copy-start | bytes 772
  15.0 18.5 %copy-start.7 = (s32[1,64,8]{1,2,0:T(8,128)S(1)}, s32[1,64,8]{1,2,0:T(8,128)}, u32[]{:S(2)}) copy-start(s32[1,64,8]{1,2,0:T(8,128)} %param.11) | copy-start | bytes 6148
  15.0 19.2 %copy-start.6 = (bf16[128,512]{1,0:T(8,128)(2,1)S(1)}, bf16[128,512]{1,0:T(8,128)(2,1)}, u32[]{:S(2)}) copy-start(bf16[128,512]{1,0:T(8,128)(2,1)} %param.7) | copy-start | bytes 393220
  15.0 180.6 %all-to-all-start = ((bf16[32,64,1024]{2,1,0:T(8,128)(2,1)}), bf16[32,64,1024]{2,1,0:T(8,128)(2,1)}, u32[]{:S(2)}, u32[]{:S(2)}) async-start(bf16[32,64,1024]{2,1,0:T(8,128)(2,1)} %bitcast.97), calls=%async_computation | async-start | bytes 8388608 | tf_op jit(solution)/shard_map/all_to_all | solution.py:39
  31.8 161.1 %all-gather.2.cloned.1.call-start = ((), (), s32[]{:S(2)}) async-start(), calls=%async_computation.3 | async-start | bytes 1081344 | tf_op jit(solution)/shard_map/all_gather | solution.py:77
  194.7 5.1 copy-start.3
  216.0 1.0 copy-start.2
  216.9 1.2 copy-start.1
  219.3 0.9 copy-start.4
  261.8 7.8 %copy-start.5 = (bf16[2,64,8,64]{1,3,2,0:T(8,128)(2,1)S(1)}, bf16[2,64,8,64]{1,3,2,0:T(8,128)(2,1)}, u32[]{:S(2)}) copy-start(bf16[2,64,8,64]{1,3,2,0:T(8,128)(2,1)} %get-tuple-element.21) | copy-start | bytes 393220
  261.8 367.1 %all-to-all-start.1 = ((bf16[32,64,1024]{2,1,0:T(8,128)(2,1)}), bf16[32,64,1024]{2,1,0:T(8,128)(2,1)}, u32[]{:S(2)}, u32[]{:S(2)}) async-start(bf16[32,64,1024]{2,1,0:T(8,128)(2,1)} %copy.47), calls=%async_computation.1 | async-start | bytes 8388608 | tf_op jit(solution)/shard_map/all_to_all | solution.py:115
  269.5 303.4 %reduce-scatter.4.cloned.1.call-start = ((), (), s32[]{:S(2)}) async-start(), calls=%async_computation.4 | async-start | bytes 1081344
  628.8 4.6 slice-start
Sparse Core Ops, SparseCore 0:
  35.8 157.0 all-gather.1
  274.7 298.1 reduce-scatter.3
where the time goes:
time: 645 us; the launch traced here: 642 us
  waiting for transfers between devices  458 us (71%)
  local copies, waits for them, and re-layouts  70.1 us (11%)
  blocking collectives  54.4 us (8%)
  starting transfers between devices  24.6 us (4%)
  between operations  15 us (2%)
  matrix products  14.6 us (2%)
    unnamed x3, waiting for transfers between devices  300 us
    all_gather x1, waiting for transfers between devices, per_device(): full_weight = lax.all_gather(out_weight, 'ctx', axis=0, tiled=True)  157 us
    psum x1, blocking collectives, per_device(): weight_grad = lax.psum(shard_sum, 'dp').astype(jnp.float32)  54.4 us
    unnamed x26, local copies, waits for them, and re-layouts  23.2 us
    all_to_all x1, starting transfers between devices, per_device(): lax.all_to_all(outgoing.reshape(ctx_ranks, BLK, width_two), 'ctx', split_...  16.8 us
  transfers between devices with their start and end apart: 4, of which 2 were waited for; matrix products, arithmetic and copies ran while one was open for 2% of the time, Pallas kernels for 0%

commit v1 on v0

v1 whole, which is shorter than its diff:
```python
import functools
import math

import jax
import jax.numpy as jnp
from jax import lax
from jax.experimental import pallas as pl
from jax.experimental.pallas import tpu as pltpu
from jax.sharding import PartitionSpec as P

HEADS = 8
HEAD_DIM = 64
BLK = 64
KPQ = 8
CTX = 32
PLANE = 8
MESH = pl.DeviceIdType.MESH
BF16 = jnp.bfloat16
F32 = jnp.float32


def to_ctx(src, dst, send, recv, peer):
    return pltpu.make_async_remote_copy(
        src_ref=src, dst_ref=dst, send_sem=send, recv_sem=recv,
        device_id={"ctx": peer}, device_id_type=MESH,
    )


def to_dp(src, dst, send, recv, peer):
    return pltpu.make_async_remote_copy(
        src_ref=src, dst_ref=dst, send_sem=send, recv_sem=recv,
        device_id={"dp": peer}, device_id_type=MESH,
    )


def low_half(shape):
    return lax.broadcasted_iota(jnp.int32, shape, 1) < HEAD_DIM


def pair_up(first, second, which):
    first, second = first.astype(F32), second.astype(F32)
    low = low_half(first.shape)
    if which == 0:
        out = jnp.where(low, first, pltpu.roll(second, HEAD_DIM, 1))
    else:
        out = jnp.where(low, pltpu.roll(first, HEAD_DIM, 1), second)
    return out


def gather_kernel(length_ref, q_ref, kv_ref, w_ref, og_ref, kv_all, qg_all,
                  kv_pack, qg_pack, w_all, w_send, w_recv, s_send, s_recv,
                  kv_send, kv_recv, qg_send, qg_recv):
    dp = lax.axis_index("dp")
    me = lax.axis_index("ctx")
    col, z = me // PLANE, lax.rem(me, PLANE)
    part = lax.rem(dp, PLANE)
    ctx_peers = [lax.rem(me + i, CTX) for i in range(1, CTX)]
    dp_peers = [dp - part + lax.rem(part + i, PLANE) for i in range(1, PLANE)]
    z_peers = [lax.rem(z + i, PLANE) for i in range(1, PLANE)]

    barrier = pltpu.get_barrier_semaphore()
    for peer in ctx_peers:
        pl.semaphore_signal(barrier, inc=1, device_id={"ctx": peer}, device_id_type=MESH)
    for peer in dp_peers:
        pl.semaphore_signal(barrier, inc=1, device_id={"dp": peer}, device_id_type=MESH)

    for head in range(HEADS):
        pair = slice(128 * (head // 2), 128 * (head // 2) + 128)
        vpair = slice(512 + 128 * (head // 2), 512 + 128 * (head // 2) + 128)
        kv_pack[head] = pair_up(kv_ref[:, pair], kv_ref[:, vpair], head % 2).astype(BF16)

    pl.semaphore_wait(barrier, CTX - 1 + PLANE - 1)

    row0 = pl.multiple_of((part // 4) * 16, 16)
    col0 = pl.multiple_of(lax.rem(part, 4) * 128, 128)
    tile = w_ref.at[pl.ds(row0, 16), pl.ds(col0, 128)]
    started = []
    w_copies = []
    for i, peer in enumerate(ctx_peers):
        w_copies.append(to_ctx(tile, w_all.at[part, me], w_send.at[i], w_recv.at[i], peer))
        w_copies[-1].start()
    w_all[part, me] = w_ref[pl.ds(row0, 16), pl.ds(col0, 128)]
    for i, peer in enumerate(ctx_peers):
        copy = to_ctx(kv_pack.at[lax.rem(peer, PLANE)], kv_all.at[me], kv_send.at[i], kv_recv.at[i], peer)
        copy.start()
        started.append(copy)
    kv_all[me] = kv_pack[z]
    for copy in w_copies:
        copy.wait()
    share = []
    for i, peer in enumerate(dp_peers):
        copy = to_dp(w_all.at[part], w_all.at[part], s_send.at[i], s_recv.at[i], peer)
        copy.start()
        share.append(copy)
    for copy in share:
        copy.wait()

    rows = me * 128 + lax.broadcasted_iota(jnp.int32, (128, 1), 0)
    valid = (rows < length_ref[0]).astype(F32)
    out_grad = og_ref[...]
    for c in range(4):
        weight = jnp.stack([w_all[c], w_all[4 + c]], axis=1).reshape(1024, 128)
        grad = jnp.dot(out_grad, weight, preferred_element_type=F32) * valid
        query = q_ref[:, 128 * c:128 * c + 128]
        qg_pack[2 * c] = pair_up(query, grad, 0).astype(BF16)
        qg_pack[2 * c + 1] = pair_up(query, grad, 1).astype(BF16)
    for i, peer in enumerate(z_peers):
        copy = to_ctx(qg_pack.at[peer], qg_all.at[z], qg_send.at[i], qg_recv.at[i], col * PLANE + peer)
        copy.start()
        started.append(copy)
    qg_all[z] = qg_pack[z]
    for copy in started:
        copy.wait()


def attention_kernel(list_ref, count_ref, info_ref, kv_ref, qg_ref, dkv_ref, dqo_ref, total):
    factor = 1.0 / math.sqrt(HEAD_DIM)
    total[...] = jnp.zeros_like(total)
    length = info_ref[0]
    first = info_ref[1]
    lane = lax.broadcasted_iota(jnp.int32, (1, 128), 1)
    low = low_half((BLK, 128))

    def unit(u, carry):
        qg = qg_ref[u].astype(F32)
        left = jnp.concatenate(
            [jnp.where(low, qg * factor, 0.0), jnp.where(low, 0.0, qg)], axis=0
        ).astype(BF16)
        blocks = [list_ref[u, j] for j in range(KPQ)]
        keyval = jnp.concatenate([kv_ref[b] for b in blocks], axis=0)
        both = lax.dot_general(left, keyval, (((1,), (1,)), ((), ())), preferred_element_type=F32)
        count = count_ref[u]
        place = jnp.concatenate(
            [
                jnp.where(lane < BLK, blocks[j] * BLK + lane, blocks[j + 1] * BLK + lane - BLK)
                for j in range(0, KPQ, 2)
            ],
            axis=1,
        )
        entry = lax.broadcasted_iota(jnp.int32, (1, KPQ * BLK), 1) // BLK
        own = (first + u) * BLK + lax.broadcasted_iota(jnp.int32, (BLK, 1), 0)
        allowed = (entry < count) & ((place < length) | (place == own))
        scores = jnp.where(allowed, both[:BLK], -jnp.inf)
        exponent = jnp.exp(scores - jnp.max(scores, axis=1, keepdims=True))
        probs = exponent * (1.0 / jnp.sum(exponent, axis=1, keepdims=True))
        probs16 = probs.astype(BF16)
        probs = probs16.astype(F32)
        prob_grad = both[BLK:]
        delta = jnp.sum(probs * prob_grad, axis=1, keepdims=True)
        score_grad = (probs * (prob_grad - delta)).astype(BF16)
        stacked = jnp.concatenate([score_grad, probs16], axis=0)
        back = jnp.dot(stacked, keyval, preferred_element_type=F32)
        valid = (own < length).astype(F32)
        dqo_ref[u] = jnp.where(low, back[:BLK] * factor, back[BLK:] * valid).astype(BF16)
        grads = lax.dot_general(stacked, left, (((0,), (0,)), ((), ())), preferred_element_type=F32)
        for j in range(KPQ):
            total[blocks[j]] += grads[j * BLK:(j + 1) * BLK]
        return carry

    lax.fori_loop(0, qg_ref.shape[0], unit, 0)
    dkv_ref[...] = total[...].astype(BF16)


def return_kernel(dkv_ref, dqo_ref, dq_out, dkv_out, attn_out, dkv_in, dqo_in,
                  kv_send, kv_recv, q_send, q_recv):
    me = lax.axis_index("ctx")
    col, z = me // PLANE, lax.rem(me, PLANE)
    ctx_peers = [lax.rem(me + i, CTX) for i in range(1, CTX)]
    z_peers = [lax.rem(z + i, PLANE) for i in range(1, PLANE)]
    barrier = pltpu.get_barrier_semaphore()
    for peer in ctx_peers:
        pl.semaphore_signal(barrier, inc=1, device_id={"ctx": peer}, device_id_type=MESH)
    pl.semaphore_wait(barrier, CTX - 1)
    q_copies, kv_copies = [], []
    for i, peer in enumerate(z_peers):
        copy = to_ctx(dqo_ref.at[peer], dqo_in.at[z], q_send.at[i], q_recv.at[i], col * PLANE + peer)
        copy.start()
        q_copies.append(copy)
    for i, peer in enumerate(ctx_peers):
        copy = to_ctx(dkv_ref.at[peer], dkv_in.at[me], kv_send.at[i], kv_recv.at[i], peer)
        copy.start()
        kv_copies.append(copy)
    dqo_in[z] = dqo_ref[z]
    dkv_in[me] = dkv_ref[me]
    for copy in q_copies:
        copy.wait()
    for c in range(4):
        even, odd = dqo_in[2 * c], dqo_in[2 * c + 1]
        cols = slice(128 * c, 128 * c + 128)
        dq_out[:, cols] = pair_up(even, odd, 0).astype(BF16)
        attn_out[:, cols] = pair_up(even, odd, 1).astype(BF16)
    for copy in kv_copies:
        copy.wait()
    for c in range(4):
        sums = []
        for head in (2 * c, 2 * c + 1):
            sums.append(sum(dkv_in[y * PLANE + head].astype(F32) for y in range(CTX // PLANE)))
        dkv_out[:, 128 * c:128 * c + 128] = pair_up(sums[0], sums[1], 0).astype(BF16)
        dkv_out[:, 512 + 128 * c:512 + 128 * c + 128] = pair_up(sums[0], sums[1], 1).astype(BF16)


def vmem(n):
    return [pl.BlockSpec(memory_space=pltpu.VMEM)] * n


def per_device(queries, keyvals, out_weight, out_grad, block_lists, block_counts, seq_lengths):
    me = lax.axis_index("ctx")
    dma = pltpu.SemaphoreType.DMA
    smem = pl.BlockSpec(memory_space=pltpu.SMEM)
    kv_all, qg_all = pl.pallas_call(
        gather_kernel,
        out_shape=(
            jax.ShapeDtypeStruct((CTX, 128, 128), BF16),
            jax.ShapeDtypeStruct((PLANE, 128, 128), BF16),
        ),
        in_specs=[smem] + vmem(4),
        out_specs=tuple(vmem(2)),
        scratch_shapes=[
            pltpu.VMEM((HEADS, 128, 128), BF16),
            pltpu.VMEM((HEADS, 128, 128), BF16),
            pltpu.VMEM((PLANE, CTX, 16, 128), BF16),
            dma((CTX - 1,)), dma((CTX - 1,)),
            dma((PLANE - 1,)), dma((PLANE - 1,)),
            dma((CTX - 1,)), dma((CTX - 1,)),
            dma((PLANE - 1,)), dma((PLANE - 1,)),
        ],
        compiler_params=pltpu.CompilerParams(
            collective_id=0, has_side_effects=True, vmem_limit_bytes=32 * 2**20
        ),
        name="gather",
    )(seq_lengths, queries, keyvals, out_weight, out_grad)

    first = (me // PLANE) * 16
    mine = lax.dynamic_slice_in_dim(block_lists[0], first, 16, 0)
    counts = lax.dynamic_slice_in_dim(block_counts[0], first, 16, 0)
    info = jnp.stack([seq_lengths[0], first])
    dkv, dqo = pl.pallas_call(
        attention_kernel,
        out_shape=(
            jax.ShapeDtypeStruct((64, BLK, 128), BF16),
            jax.ShapeDtypeStruct((16, BLK, 128), BF16),
        ),
        in_specs=[smem] * 3 + vmem(2),
        out_specs=tuple(vmem(2)),
        scratch_shapes=[pltpu.VMEM((64, BLK, 128), F32)],
        compiler_params=pltpu.CompilerParams(vmem_limit_bytes=32 * 2**20),
        name="attention",
    )(mine, counts, info, kv_all.reshape(64, BLK, 128), qg_all.reshape(16, BLK, 128))

    query_grad, keyval_grad, attention_rows = pl.pallas_call(
        return_kernel,
        out_shape=(
            jax.ShapeDtypeStruct((128, 512), BF16),
            jax.ShapeDtypeStruct((128, 1024), BF16),
            jax.ShapeDtypeStruct((128, 512), BF16),
        ),
        in_specs=vmem(2),
        out_specs=tuple(vmem(3)),
        scratch_shapes=[
            pltpu.VMEM((CTX, 128, 128), BF16),
            pltpu.VMEM((PLANE, 128, 128), BF16),
            dma((CTX - 1,)), dma((CTX - 1,)),
            dma((PLANE - 1,)), dma((PLANE - 1,)),
        ],
        compiler_params=pltpu.CompilerParams(
            collective_id=1, has_side_effects=True, vmem_limit_bytes=32 * 2**20
        ),
        name="giveback",
    )(dkv.reshape(CTX, 128, 128), dqo.reshape(PLANE, 128, 128))

    groups = lax.axis_size("dp")
    scaling = 1.0 / math.sqrt(128 * CTX * groups)
    shard_sum = lax.psum_scatter(
        (
            lax.dot_general(
                out_grad, attention_rows, (((0,), (0,)), ((), ())), preferred_element_type=F32
            )
            * scaling
        ).astype(BF16),
        "ctx",
        scatter_dimension=0,
        tiled=True,
    )
    weight_grad = lax.psum(shard_sum, "dp").astype(F32)
    return (query_grad, keyval_grad, weight_grad)


def solution(mesh):
    placed = (
        P(("dp", "ctx"), None),
        P(("dp", "ctx"), None),
        P("ctx", None),
        P(("dp", "ctx"), None),
        P("dp", None, None),
        P("dp", None),
        P("dp"),
    )
    return jax.shard_map(
        per_device,
        mesh=mesh,
        in_specs=placed,
        out_specs=(P(("dp", "ctx"), None), P(("dp", "ctx"), None), P("ctx", None)),
        check_vma=False,
    )
```

time: 645 us -> 422 us (0.65)
  waiting for transfers between devices: 458 us -> 220 us
  Pallas kernels: 0 us -> 120 us
  local copies, waits for them, and re-layouts: 70.1 us -> 8.72 us
  starting transfers between devices: 24.6 us -> 0.04 us
  matrix products: 14.6 us -> 0.46 us
    all_gather x1 -> x0, waiting for transfers between devices: 157 us -> none  [per_device(): full_weight = lax.all_gather(out_weight, 'ctx', axis=0, tiled=True)]
    pallas_call x0 -> x3, Pallas kernels: none -> 120 us  [the longest x1 65.2 us: per_device(): pl.pallas_call(gather_kernel, out_shape=(jax.ShapeDtypeStruct((CTX, 128,...]
    unnamed x3 -> x2, waiting for transfers between devices: 300 us -> 220 us
    all_to_all x2 -> x0, starting transfers between devices: 24.5 us -> none  [the longest x1 16.8 us: per_device(): lax.all_to_all(outgoing.reshape(ctx_ranks, BLK, width_two), 'ctx', split_...]
    reshape x10 -> x0, local copies, waits for them, and re-layouts: 19.3 us -> none  [the longest x1 6 us: per_device(): jnp.stack([key_grad, value_grad], axis=2)]
    unnamed x26 -> x15, local copies, waits for them, and re-layouts: 23.2 us -> 7.85 us
    dot_general x9 -> x0, matrix products: 12.3 us -> none  [the longest x1 5.78 us: per_device(): jnp.dot(owner_table, remote_terms, precision=lax.Precision.HIGHEST, prefe...]
    slice x4 -> x0, local copies, waits for them, and re-layouts: 8.29 us -> none  [the longest x1 4.48 us: per_device(): entry_grads[:, 1:].reshape(blocks_here * (KPQ - 1), BLK * width_two)]
  transfers between devices with their start and end apart: 4 -> 1, of which waited for: 2 -> 1; matrix products, arithmetic and copies ran while one was open for 2% -> 0% of each run, Pallas kernels for 0% -> 0%
where the time goes in v1:
time: 422 us; the launch traced here: 419 us
  waiting for transfers between devices  220 us (52%)
  Pallas kernels  120 us (28%)
  blocking collectives  54.3 us (13%)
  between operations  14.7 us (3%)
  local copies, waits for them, and re-layouts  8.72 us (2%)
    unnamed x2, waiting for transfers between devices  220 us
    pallas_call x1, Pallas kernels, per_device(): pl.pallas_call(gather_kernel, out_shape=(jax.ShapeDtypeStruct((CTX, 128,...  65.2 us
    psum x1, blocking collectives, per_device(): weight_grad = lax.psum(shard_sum, 'dp').astype(F32)  54.3 us
    pallas_call x1, Pallas kernels, per_device(): pl.pallas_call(return_kernel, out_shape=(jax.ShapeDtypeStruct((128, 512),...  42.7 us
    pallas_call x1, Pallas kernels, per_device(): pl.pallas_call(attention_kernel, out_shape=(jax.ShapeDtypeStruct((64, BLK...  12.3 us
  transfers between devices with their start and end apart: 1, of which 1 were waited for; matrix products, arithmetic and copies ran while one was open for 0% of the time, Pallas kernels for 0%

profile of v1, /device:TPU:1, one launch (start us, length us, event | category | flops | bytes accessed | tf_op | source)
XLA Modules:
  0.0 418.6 jit_solution(13398209637227268598)
XLA Ops:
  7.2 0.0 copy-start
  7.2 0.0 reduce-scatter.4.cloned.1.call-start
  7.9 0.7 dynamic-slice_bitcast_fusion.1.count_ref
  8.6 0.0 copy-done
  8.6 0.1 dynamic-slice_bitcast_fusion
  8.7 0.1 copy.12.list_ref
  8.8 0.1 pad_add_fusion.info_ref
  8.8 0.0 copy-start.1
  8.9 0.9 copy-done.1
  9.8 0.0 copy-start.2
  9.8 0.9 copy-done.2
  10.8 0.0 copy-start.3
  10.8 0.9 copy-done.3
  11.7 0.0 copy-start.4
  11.7 0.8 copy-done.4
  12.4 65.2 %gather.1 = (bf16[32,128,128]{2,1,0:T(8,128)(2,1)S(1)}, bf16[8,128,128]{2,1,0:T(8,128)(2,1)S(1)}) custom-call(s32[1]{0:T(128)S(6)} %copy.18.length_ref, bf16[128,512]{1,0:T(8,128)(2,1)S(1)} %copy-done.3, bf16[128,1024]{1,0:T(8,128)(2,1)S(1)} %copy-done.2, bf16[32,512]{1,0:T(8,128)(2,1)S(1)} %copy-done.4, bf16[128,1024]{1,0:T(8,128)(2,1)S(1)} %copy-done.1), custom_call_target="tpu_custom_call" | custom-call | tf_op jit(solution)/shard_map/gather/pallas_call | solution.py:210
  77.7 12.3 %attention.1 = (bf16[64,64,128]{2,1,0:T(8,128)(2,1)S(1)}, bf16[16,64,128]{2,1,0:T(8,128)(2,1)S(1)}) custom-call(s32[16,8]{1,0:T(8,128)S(1)} %copy.12.list_ref, s32[16]{0:T(128)S(1)} %dynamic-slice_bitcast_fusion.1.count_ref, s32[2]{0:T(128)S(1)} %pad_add_fusion.info_ref, bf16[64,64,128]{2,1,0:T(8,128)(2,1)S(1)} %bitcast.15, bf16[16,64,128]{2,1,0:T(8,128)(2,1)S(1)} %bitcast.17), custom_call_target="tpu_custom_call" | custom-call | tf_op jit(solution)/shard_map/attention/pallas_call | solution.py:237
  90.0 42.7 %giveback.1 = (bf16[128,512]{1,0:T(8,128)(2,1)S(1)}, bf16[128,1024]{1,0:T(8,128)(2,1)S(1)}, bf16[128,512]{1,0:T(8,128)(2,1)S(1)}) custom-call(bf16[32,128,128]{2,1,0:T(8,128)(2,1)S(1)} %bitcast.14, bf16[8,128,128]{2,1,0:T(8,128)(2,1)S(1)} %bitcast.16), custom_call_target="tpu_custom_call" | custom-call | tf_op jit(solution)/shard_map/giveback/pallas_call | solution.py:250
  132.7 0.5 fusion
  133.2 1.3 copy.14
  134.5 0.0 reduce-scatter.4.cloned.1.call-update
  134.5 219.9 %reduce-scatter.4.cloned.1.call-done = bf16[32,512]{1,0:T(8,128)(2,1)} async-done(((bf16[1024,512]{1,0:T(8,128)(2,1)}), bf16[32,512]{1,0:T(8,128)(2,1)}) %reduce-scatter.4.cloned.1.call-update) | async-done | bytes 32784
  354.4 0.9 copy.15
  355.3 54.3 %psum.7 = bf16[32,512]{0,1:T(8,128)(2,1)S(1)} all-reduce(bf16[32,512]{0,1:T(8,128)(2,1)S(1)} %copy.15), channel_id=1, replica_groups=mesh['dp'=16,'ctx'=32] {'dp'}, use_global_device_ids=true, to_apply=%region_1.2 | all-reduce | flops 16384 | bytes 65536 | tf_op jit(solution)/shard_map/psum | solution.py:284
  409.6 0.7 copy.13
  410.4 0.7 copy.19
  411.0 0.7 copy.20
Async XLA Ops:
  7.2 1.5 copy-start
  7.2 347.3 %reduce-scatter.4.cloned.1.call-start = ((), (), s32[]{:S(2)}) async-start(), calls=%async_computation.1 | async-start | bytes 1081344
  8.8 1.0 copy-start.1
  9.8 0.9 copy-start.2
  10.8 0.9 copy-start.3
  11.7 0.8 copy-start.4
Sparse Core Ops, SparseCore 0:
  134.7 219.7 reduce-scatter.3

commit v2 on v0

v2 whole, which is shorter than its diff:
```python
import math

import jax
import jax.numpy as jnp
from jax import lax
from jax.experimental import pallas as pl
from jax.experimental.pallas import tpu as pltpu
from jax.sharding import PartitionSpec as P

HEADS = 8
HEAD_DIM = 64
BLK = 64
KPQ = 8
NQB = 64
CTX = 32
DP = 16
PLANE = 8
UNITS = 16
ENTRIES = UNITS * KPQ
FACTOR = 1.0 / math.sqrt(HEAD_DIM)
WG_SCALE = 1.0 / math.sqrt(128 * CTX * DP)
MESH = pl.DeviceIdType.MESH
BF16 = jnp.bfloat16
F32 = jnp.float32

T_LIST = 0
T_PERM = T_LIST + ENTRIES
T_SAME = T_PERM + ENTRIES
T_LAST = T_SAME + ENTRIES
T_COUNT = T_LAST + NQB
T_LENGTH = T_COUNT + UNITS


def low_half(shape):
    return lax.broadcasted_iota(jnp.int32, shape, 1) < HEAD_DIM


def pair_up(first, second, which):
    first, second = first.astype(F32), second.astype(F32)
    low = low_half(first.shape)
    if which == 0:
        return jnp.where(low, first, pltpu.roll(second, HEAD_DIM, 1))
    return jnp.where(low, pltpu.roll(first, HEAD_DIM, 1), second)


def dot(a, b, dims=((1,), (0,))):
    return lax.dot_general(a, b, (dims, ((), ())), preferred_element_type=F32)


def remote(src, dst, send, recv, **where):
    return pltpu.make_async_remote_copy(
        src_ref=src, dst_ref=dst, send_sem=send, recv_sem=recv,
        device_id=where, device_id_type=MESH,
    )


def body(tab, q_hbm, kv_hbm, w_hbm, og_hbm, dq_out, dkv_out, wg_out,
         q_ref, kv_ref, w_ref, w_tile, w_all, og_all, og_t, q_pack, q_all, kv_pack, kv_all,
         g_pack, g_all, p_all, o_pack, o_all, dq_pack, dq_all, entry_grads, sums,
         dkv_pack, dkv_in, wg_pack, wg_in, wg_last, wg_all,
         in_sem, w_s, w_r, og_s, og_r, oc_s, oc_r, q_s, q_r, kv_s, kv_r, g_s, g_r,
         o_s, o_r, dq_s, dq_r, dkv_s, dkv_r, b_s, b_r, c_s, c_r):
    dp = lax.axis_index("dp")
    me = lax.axis_index("ctx")
    col, z = me // PLANE, lax.rem(me, PLANE)
    part = lax.rem(dp, PLANE)
    base = dp - part
    x, core = part // 2, lax.rem(part, 2)
    partner = base + 2 * x + 1 - core
    ctx_peers = [lax.rem(me + i, CTX) for i in range(1, CTX)]
    dp_peers = [lax.rem(dp + i, DP) for i in range(1, DP)]
    z_peers = [lax.rem(z + i, PLANE) for i in range(1, PLANE)]
    x_peers = [lax.rem(x + i, 4) for i in range(1, 4)]
    here = part == z

    loads = [
        pltpu.make_async_copy(w_hbm, w_ref, in_sem.at[0]),
        pltpu.make_async_copy(og_hbm, og_all.at[part], in_sem.at[1]),
        pltpu.make_async_copy(q_hbm, q_ref, in_sem.at[2]),
        pltpu.make_async_copy(kv_hbm, kv_ref, in_sem.at[3]),
    ]
    for copy in loads:
        copy.start()

    barrier = pltpu.get_barrier_semaphore()

    def greet(**where):
        pl.semaphore_signal(barrier, inc=1, device_id=where, device_id_type=MESH)

    for peer in ctx_peers:
        greet(ctx=peer)
    for peer in dp_peers:
        greet(dp=peer)
    for i in range(1, PLANE):
        greet(dp=base + z, ctx=col * PLANE + lax.rem(z + i, PLANE))
        greet(dp=base + lax.rem(part + i, PLANE), ctx=col * PLANE + part)

    @pl.when(jnp.logical_not(here))
    def _():
        greet(dp=base + z, ctx=me)
        greet(dp=dp, ctx=col * PLANE + part)

    low16 = low_half((16, 128))
    low = low_half((BLK, 128))
    loads[0].wait()
    pair = w_ref[:, pl.ds(pl.multiple_of(128 * (part // 2), 128), 128)]
    odd = (lax.rem(part, 2) == 1).astype(F32)
    tile = pair_up(pair[:16], pair[16:], 0) * (1.0 - odd) + pair_up(pair[:16], pair[16:], 1) * odd
    w_tile[...] = tile.astype(BF16)
    w_all[me] = tile.astype(BF16)
    loads[2].wait()
    for head in range(HEADS):
        cols = slice(128 * (head // 2), 128 * (head // 2) + 128)
        q_pack[head] = pair_up(q_ref[:BLK, cols], q_ref[BLK:, cols], head % 2).astype(BF16)
    loads[3].wait()
    for head in range(HEADS):
        first = 128 * (head // 2)
        for half in range(2):
            rows = slice(BLK * half, BLK * half + BLK)
            kv_pack[head, half] = pair_up(
                kv_ref[rows, first:first + 128], kv_ref[rows, 512 + first:640 + first], head % 2
            ).astype(BF16)
    loads[1].wait()

    barrier_count = CTX - 1 + DP - 1 + 2 * (PLANE - 1) + jnp.where(here, 0, 2)
    pl.semaphore_wait(barrier, barrier_count)

    w_copies, og_copies, og_core, q_copies, kv_copies = [], [], [], [], []
    for i, peer in enumerate(ctx_peers):
        w_copies.append(remote(w_tile, w_all.at[me], w_s.at[i], w_r.at[i], ctx=peer))
    for i, peer in enumerate(x_peers):
        mine = og_all.at[part]
        og_copies.append(
            remote(mine, mine, og_s.at[i], og_r.at[i], dp=base + 2 * peer + core)
        )
    og_core.append(remote(og_all.at[part], og_all.at[part], oc_s.at[3], oc_r.at[3], dp=partner))
    for i, peer in enumerate(z_peers):
        q_copies.append(
            remote(q_pack.at[peer], q_all.at[z], q_s.at[i], q_r.at[i], ctx=col * PLANE + peer)
        )
    for i, peer in enumerate(ctx_peers):
        kv_copies.append(
            remote(kv_pack.at[lax.rem(peer, PLANE)], kv_all.at[pl.ds(2 * me, 2)],
                   kv_s.at[i], kv_r.at[i], ctx=peer)
        )
    for copy in w_copies + og_copies + og_core + q_copies + kv_copies:
        copy.start()
    q_all[z] = q_pack[z]
    kv_all[pl.ds(2 * me, 2)] = kv_pack[z]

    for i in range(3):
        og_copies[i].wait_recv()
        slot = 2 * lax.rem(x + 3 - i, 4) + core
        copy = remote(og_all.at[slot], og_all.at[slot], oc_s.at[i], oc_r.at[i], dp=partner)
        copy.start()
        og_core.append(copy)
    for copy in w_copies:
        copy.wait()
    for copy in og_core:
        copy.wait_recv()

    weight = w_all[...].reshape(CTX, 1, 16, 128)
    none = jnp.zeros_like(weight)
    low4 = lax.broadcasted_iota(jnp.int32, weight.shape, 3) < HEAD_DIM
    weight = jnp.concatenate(
        [jnp.where(low4, weight, none), jnp.where(low4, none, weight)], axis=1
    ).reshape(CTX * 32, 128)
    for s in range(PLANE):
        grad = dot(og_all[s], weight)
        grad = grad + pltpu.roll(grad, HEAD_DIM, 1)
        g_pack[s] = jnp.where(low, grad[:BLK], grad[BLK:]).astype(BF16)
    g_copies = []
    for i in range(PLANE):
        peer = lax.rem(part + i, PLANE)
        copy = remote(g_pack.at[peer], g_all.at[z], g_s.at[i], g_r.at[z],
                      dp=base + peer, ctx=col * PLANE + part)
        g_copies.append(copy)
        if i:
            copy.start()
        else:
            pl.when(jnp.logical_not(here))(copy.start)

            @pl.when(here)
            def _():
                g_all[z] = g_pack[part]

    for s in range(PLANE):
        og_t[:, 128 * s:128 * s + 128] = og_all[s].T
    for copy in q_copies + kv_copies:
        copy.wait_recv()

    length = tab[T_LENGTH]
    lane = lax.broadcasted_iota(jnp.int32, (1, 128), 1)
    row = lax.broadcasted_iota(jnp.int32, (BLK, 1), 0)
    entry = lax.broadcasted_iota(jnp.int32, (1, KPQ * BLK), 1) // BLK

    def listed(u):
        blocks = [tab[T_LIST + u * KPQ + j] for j in range(KPQ)]
        return blocks, jnp.concatenate([kv_all[b] for b in blocks], axis=0)

    def forward(zp, carry):
        query = q_all[zp].astype(F32) * FACTOR
        outs = []
        for p in range(2):
            u = 2 * zp + p
            blocks, keyval = listed(u)
            left = query if p == 0 else pltpu.roll(query, HEAD_DIM, 1)
            scores = dot(jnp.where(low, left, 0.0).astype(BF16), keyval, ((1,), (1,)))
            place = jnp.concatenate(
                [
                    jnp.where(lane < BLK, blocks[j] * BLK + lane, blocks[j + 1] * BLK + lane - BLK)
                    for j in range(0, KPQ, 2)
                ],
                axis=1,
            )
            own = (col * UNITS + u) * BLK + row
            allowed = (entry < tab[T_COUNT + u]) & ((place < length) | (place == own))
            scores = jnp.where(allowed, scores, -jnp.inf)
            exponent = jnp.exp(scores - jnp.max(scores, axis=1, keepdims=True))
            probs = exponent * (1.0 / jnp.sum(exponent, axis=1, keepdims=True))
            probs = probs.astype(BF16)
            p_all[u] = probs
            outs.append(dot(probs, keyval) * (own < length).astype(F32))
        o_pack[zp] = pair_up(outs[0], outs[1], 1).astype(BF16)
        return carry

    lax.fori_loop(0, PLANE, forward, 0)

    o_copies = []
    for i in range(PLANE):
        peer = lax.rem(z + i, PLANE)
        copy = remote(o_pack.at[peer], o_all.at[part], o_s.at[i], o_r.at[part],
                      dp=base + z, ctx=col * PLANE + peer)
        o_copies.append(copy)
        if i:
            copy.start()
        else:
            pl.when(jnp.logical_not(here))(copy.start)

            @pl.when(here)
            def _():
                o_all[part] = o_pack[z]

    def arrived(dst, sem):
        remote(dst, dst, sem, sem, dp=dp, ctx=me).wait_recv()

    for i in range(1, PLANE):
        slot = lax.rem(z + i, PLANE)
        arrived(g_all.at[slot], g_r.at[slot])

    @pl.when(jnp.logical_not(here))
    def _():
        arrived(g_all.at[z], g_r.at[z])

    def backward(zp, carry):
        query = q_all[zp].astype(F32) * FACTOR
        grads = g_all[zp].astype(F32)
        outs = []
        for p in range(2):
            u = 2 * zp + p
            _, keyval = listed(u)
            valid = ((col * UNITS + u) * BLK + row < length).astype(F32)
            if p == 0:
                top, bottom = query, pltpu.roll(grads, HEAD_DIM, 1)
            else:
                top, bottom = pltpu.roll(query, HEAD_DIM, 1), grads
            top = jnp.where(low, top, 0.0).astype(BF16)
            bottom = jnp.where(low, 0.0, bottom * valid).astype(BF16)
            prob_grad = dot(bottom, keyval, ((1,), (1,)))
            probs16 = p_all[u]
            probs = probs16.astype(F32)
            delta = jnp.sum(probs * prob_grad, axis=1, keepdims=True)
            score_grad = (probs * (prob_grad - delta)).astype(BF16)
            outs.append(dot(score_grad, keyval) * FACTOR)
            stacked = jnp.concatenate([score_grad, probs16], axis=0)
            grad = dot(stacked, jnp.concatenate([top, bottom], axis=0), ((0,), (0,)))
            for j in range(KPQ):
                entry_grads[u * KPQ + j] = grad[j * BLK:(j + 1) * BLK]
        dq_pack[zp] = pair_up(outs[0], outs[1], 0).astype(BF16)
        return carry

    lax.fori_loop(0, PLANE, backward, 0)

    dq_copies = []
    for i, peer in enumerate(z_peers):
        copy = remote(dq_pack.at[peer], dq_all.at[z], dq_s.at[i], dq_r.at[i], ctx=col * PLANE + peer)
        copy.start()
        dq_copies.append(copy)
    dq_all[z] = dq_pack[z]

    for i in range(1, PLANE):
        slot = lax.rem(part + i, PLANE)
        arrived(o_all.at[slot], o_r.at[slot])

    @pl.when(jnp.logical_not(here))
    def _():
        arrived(o_all.at[part], o_r.at[part])

    attention = o_all[...].reshape(PLANE, 1, BLK, 128)
    none = jnp.zeros_like(attention)
    low4 = lax.broadcasted_iota(jnp.int32, attention.shape, 3) < HEAD_DIM
    attention = jnp.concatenate(
        [jnp.where(low4, attention, none), jnp.where(low4, none, attention)], axis=1
    ).reshape(PLANE * 128, 128)
    for c in range(0, CTX, 8):
        grad = dot(og_t[32 * c:32 * c + 256], attention)
        grad = ((grad + pltpu.roll(grad, HEAD_DIM, 1)) * WG_SCALE).reshape(8, 2, 16, 128)
        for k in range(8):
            wg_pack[c + k] = jnp.where(low16, grad[k, 0], grad[k, 1]).astype(BF16)
    b_copies = []
    for i, peer in enumerate(ctx_peers):
        copy = remote(wg_pack.at[peer], wg_in.at[me], b_s.at[i], b_r.at[i], ctx=peer)
        copy.start()
        b_copies.append(copy)
    wg_in[me] = wg_pack[me]

    sums[ENTRIES] = jnp.zeros((BLK, 128), F32)

    def accumulate(t, total):
        total = entry_grads[tab[T_PERM + t]] + total * tab[T_SAME + t].astype(F32)
        sums[t] = total
        return total

    lax.fori_loop(0, ENTRIES, accumulate, jnp.zeros((BLK, 128), F32), unroll=4)

    def pack(c, carry):
        for half in range(2):
            dkv_pack[c, half] = sums[tab[T_LAST + 2 * c + half]].astype(BF16)
        return carry

    lax.fori_loop(0, CTX, pack, 0, unroll=2)
    dkv_copies = []
    for i, peer in enumerate(ctx_peers):
        copy = remote(dkv_pack.at[peer], dkv_in.at[me], dkv_s.at[i], dkv_r.at[i], ctx=peer)
        copy.start()
        dkv_copies.append(copy)
    dkv_in[me] = dkv_pack[me]

    for copy in b_copies:
        copy.wait()
    wg_last[...] = sum(wg_in[i].astype(F32) for i in range(CTX)).astype(BF16)
    c_copies = []
    for i, peer in enumerate(dp_peers):
        copy = remote(wg_last, wg_all.at[dp], c_s.at[i], c_r.at[i], dp=peer)
        copy.start()
        c_copies.append(copy)
    wg_all[dp] = wg_last[...]

    for copy in dq_copies:
        copy.wait()
    for c in range(4):
        for half in range(2):
            dq_out[BLK * half:BLK * half + BLK, 128 * c:128 * c + 128] = pair_up(
                dq_all[2 * c], dq_all[2 * c + 1], half
            ).astype(BF16)

    for copy in c_copies:
        copy.wait()
    for c in range(4):
        even = wg_all[2 * c].astype(F32) + wg_all[PLANE + 2 * c].astype(F32)
        odd_ = wg_all[2 * c + 1].astype(F32) + wg_all[PLANE + 2 * c + 1].astype(F32)
        for half in range(2):
            wg_out[16 * half:16 * half + 16, 128 * c:128 * c + 128] = pair_up(even, odd_, half)

    for copy in dkv_copies:
        copy.wait()
    for c in range(4):
        for half in range(2):
            rows = slice(BLK * half, BLK * half + BLK)
            even, odd_ = [
                sum(dkv_in[y * PLANE + head, half].astype(F32) for y in range(CTX // PLANE))
                for head in (2 * c, 2 * c + 1)
            ]
            dkv_out[rows, 128 * c:128 * c + 128] = pair_up(even, odd_, 0).astype(BF16)
            dkv_out[rows, 512 + 128 * c:640 + 128 * c] = pair_up(even, odd_, 1).astype(BF16)

    for copy in og_copies + og_core + q_copies + kv_copies + g_copies[1:] + o_copies[1:]:
        copy.wait_send()

    @pl.when(jnp.logical_not(here))
    def _():
        g_copies[0].wait_send()
        o_copies[0].wait_send()


def table(block_list, counts, length, first):
    mine = lax.dynamic_slice_in_dim(block_list, first, UNITS, 0).reshape(ENTRIES)
    ids = jnp.arange(ENTRIES, dtype=jnp.int32)
    key = mine * ENTRIES + ids
    place = jnp.sum((key[None, :] < key[:, None]).astype(jnp.int32), axis=1)
    at = place[None, :] == ids[:, None]
    perm = jnp.sum(jnp.where(at, ids[None, :], 0), axis=1)
    same = (mine[None, :] == mine[:, None]) & (ids[None, :] < ids[:, None])
    later = jnp.max(same.astype(jnp.int32), axis=1)
    go_on = jnp.sum(jnp.where(at, later[None, :], 0), axis=1)
    blocks = jnp.arange(NQB, dtype=jnp.int32)
    upto = jnp.sum((mine[None, :] <= blocks[:, None]).astype(jnp.int32), axis=1)
    named = jnp.max((mine[None, :] == blocks[:, None]).astype(jnp.int32), axis=1)
    last = jnp.where(named > 0, upto - 1, ENTRIES)
    mine_counts = lax.dynamic_slice_in_dim(counts, first, UNITS, 0)
    return jnp.concatenate([mine, perm, go_on, last, mine_counts, length])


def per_device(queries, keyvals, out_weight, out_grad, block_lists, block_counts, seq_lengths):
    first = (lax.axis_index("ctx") // PLANE) * UNITS
    tab = table(block_lists[0], block_counts[0], seq_lengths, first)
    dma = pltpu.SemaphoreType.DMA
    vm = pltpu.VMEM
    any_space = pl.BlockSpec(memory_space=pl.ANY)
    pairs = [CTX - 1, 3, 4, PLANE - 1, CTX - 1, PLANE, PLANE, PLANE - 1, CTX - 1, CTX - 1, DP - 1]
    return pl.pallas_call(
        body,
        out_shape=(
            jax.ShapeDtypeStruct((128, 512), BF16),
            jax.ShapeDtypeStruct((128, 1024), BF16),
            jax.ShapeDtypeStruct((32, 512), F32),
        ),
        in_specs=[pl.BlockSpec(memory_space=pltpu.SMEM)] + [any_space] * 4,
        out_specs=tuple([pl.BlockSpec(memory_space=pltpu.VMEM)] * 3),
        scratch_shapes=[
            vm((128, 512), BF16), vm((128, 1024), BF16), vm((32, 512), BF16),
            vm((16, 128), BF16), vm((CTX, 16, 128), BF16),
            vm((PLANE, 128, 1024), BF16), vm((1024, 1024), BF16),
            vm((HEADS, BLK, 128), BF16), vm((PLANE, BLK, 128), BF16),
            vm((HEADS, 2, BLK, 128), BF16), vm((NQB, BLK, 128), BF16),
            vm((PLANE, BLK, 128), BF16), vm((PLANE, BLK, 128), BF16),
            vm((UNITS, BLK, KPQ * BLK), BF16),
            vm((PLANE, BLK, 128), BF16), vm((PLANE, BLK, 128), BF16),
            vm((PLANE, BLK, 128), BF16), vm((PLANE, BLK, 128), BF16),
            vm((ENTRIES, BLK, 128), F32), vm((ENTRIES + 1, BLK, 128), F32),
            vm((CTX, 2, BLK, 128), BF16), vm((CTX, 2, BLK, 128), BF16),
            vm((CTX, 16, 128), BF16), vm((CTX, 16, 128), BF16),
            vm((16, 128), BF16), vm((DP, 16, 128), BF16),
            dma((4,)),
        ] + [dma((n,)) for n in pairs for _ in range(2)],
        compiler_params=pltpu.CompilerParams(
            collective_id=0, has_side_effects=True, vmem_limit_bytes=48 * 2**20
        ),
        name="attention_step",
    )(tab, queries, keyvals, out_weight, out_grad)


def solution(mesh):
    placed = (
        P(("dp", "ctx"), None),
        P(("dp", "ctx"), None),
        P("ctx", None),
        P(("dp", "ctx"), None),
        P("dp", None, None),
        P("dp", None),
        P("dp"),
    )
    return jax.shard_map(
        per_device,
        mesh=mesh,
        in_specs=placed,
        out_specs=(P(("dp", "ctx"), None), P(("dp", "ctx"), None), P("ctx", None)),
        check_vma=False,
    )
```

time: 645 us -> 118 us (0.18)
  waiting for transfers between devices: 458 us -> 0 us
  Pallas kernels: 0 us -> 111 us
  local copies, waits for them, and re-layouts: 70.1 us -> 5.21 us
  blocking collectives: 54.4 us -> 0 us
  starting transfers between devices: 24.6 us -> 0 us
  matrix products: 14.6 us -> 0 us
  between operations: 15 us -> 1.37 us
    unnamed x3 -> x0, waiting for transfers between devices: 300 us -> none
    all_gather x1 -> x0, waiting for transfers between devices: 157 us -> none  [per_device(): full_weight = lax.all_gather(out_weight, 'ctx', axis=0, tiled=True)]
    pallas_call x0 -> x1, Pallas kernels: none -> 111 us  [per_device(): pl.pallas_call(body, out_shape=(jax.ShapeDtypeStruct((128, 512), BF16), j...]
    psum x1 -> x0, blocking collectives: 54.4 us -> none  [per_device(): weight_grad = lax.psum(shard_sum, 'dp').astype(jnp.float32)]
    all_to_all x2 -> x0, starting transfers between devices: 24.5 us -> none  [the longest x1 16.8 us: per_device(): lax.all_to_all(outgoing.reshape(ctx_ranks, BLK, width_two), 'ctx', split_...]
    reshape x10 -> x1, local copies, waits for them, and re-layouts: 19.3 us -> 0.09 us  [table(): lax.dynamic_slice_in_dim(block_list, first, UNITS, 0).reshape(ENTRIES)]
    unnamed x26 -> x15, local copies, waits for them, and re-layouts: 23.2 us -> 4.81 us
    dot_general x10 -> x0, matrix products: 12.8 us -> none  [the longest x1 5.78 us: per_device(): jnp.dot(owner_table, remote_terms, precision=lax.Precision.HIGHEST, prefe...]
  transfers between devices with their start and end apart: 4 -> 0, of which waited for: 2 -> 0; matrix products, arithmetic and copies ran while one was open for 2% -> 0% of each run, Pallas kernels for 0% -> 0%
where the time goes in v2:
time: 118 us
  Pallas kernels  111 us (94%)
  local copies, waits for them, and re-layouts  5.21 us (4%)
  between operations  1.37 us (1%)
    pallas_call x1, Pallas kernels, per_device(): pl.pallas_call(body, out_shape=(jax.ShapeDtypeStruct((128, 512), BF16), j...  111 us
    unnamed x15, local copies, waits for them, and re-layouts  4.81 us

profile of v2, /device:TPU:1, one launch (start us, length us, event | category | flops | bytes accessed | tf_op | source)
XLA Modules:
  0.0 117.6 jit_solution(16374614780622817587)
XLA Ops:
  0.6 0.0 copy-start
  0.7 0.0 copy-start.5
  0.7 0.0 copy-start.4
  1.3 0.0 copy-done.5
  1.3 0.1 dynamic-slice_bitcast_fusion
  1.4 0.0 copy-done
  1.4 0.1 constant_dynamic-slice_fusion
  1.5 0.1 copy.12
  1.6 0.1 reshape.36
  1.7 0.2 convert_reduce_fusion
  1.9 0.1 select_reduce_fusion
  2.0 0.1 convert_reduce_fusion.2
  2.1 0.1 concatenate.3.tab
  2.2 0.0 copy-done.4
  2.2 0.0 copy-start.1
  2.2 0.9 copy-done.1
  3.1 0.0 copy-start.2
  3.1 0.9 copy-done.2
  4.1 0.0 copy-start.3
  4.1 0.9 copy-done.3
  5.0 110.6 %attention_step.1 = (bf16[128,512]{1,0:T(8,128)(2,1)S(1)}, bf16[128,1024]{1,0:T(8,128)(2,1)S(1)}, f32[32,512]{1,0:T(8,128)S(1)}) custom-call(s32[465]{0:T(512)S(1)} %concatenate.3.tab, bf16[128,512]{1,0:T(8,128)(2,1)S(1)} %copy-done.3, bf16[128,1024]{1,0:T(8,128)(2,1)S(1)} %copy-done.1, bf16[32,512]{1,0:T(8,128)(2,1)S(1)} %copy-done.4, ...), custom_call_target="tpu_custom_call" | custom-call | tf_op jit(solution)/shard_map/attention_step/pallas_call | solution.py:411
  115.6 0.7 copy.17
  116.3 0.7 copy.18
  117.0 0.6 copy.19
  (2 shorter events, 0.0 us)
Async XLA Ops:
  0.6 0.8 copy-start
  0.7 0.7 copy-start.5
  0.7 1.5 %copy-start.4 = (bf16[32,512]{1,0:T(8,128)(2,1)S(1)}, bf16[32,512]{1,0:T(8,128)(2,1)}, u32[]{:S(2)}) copy-start(bf16[32,512]{1,0:T(8,128)(2,1)} %w_hbm.1) | copy-start | bytes 98308
  2.2 1.0 copy-start.1
  3.1 0.9 copy-start.2
  4.1 0.9 copy-start.3

commit v3 on v2

--- a/solution.py
+++ b/solution.py
@@ -13,6 +13,8 @@
 KPQ = 8
 NQB = 64
 CTX = 32
+COLS = 4
+LAG = 2
 DP = 16
 PLANE = 8
 UNITS = 16
@@ -57,9 +59,10 @@
 def body(tab, q_hbm, kv_hbm, w_hbm, og_hbm, dq_out, dkv_out, wg_out,
          q_ref, kv_ref, w_ref, w_tile, w_all, og_all, og_t, q_pack, q_all, kv_pack, kv_all,
          g_pack, g_all, p_all, o_pack, o_all, dq_pack, dq_all, entry_grads, sums,
-         dkv_pack, dkv_in, wg_pack, wg_in, wg_last, wg_all,
-         in_sem, w_s, w_r, og_s, og_r, oc_s, oc_r, q_s, q_r, kv_s, kv_r, g_s, g_r,
-         o_s, o_r, dq_s, dq_r, dkv_s, dkv_r, b_s, b_r, c_s, c_r):
+         dkv_pack, dkv_y, dkv_z, dkv_in, wg_pack, wg_in, wg_mid, wg_col, wg_last, wg_all,
+         in_sem, w_s, w_r, wy_s, wy_r, og_s, og_r, oc_s, oc_r, q_s, q_r, kv_s, kv_r, kvy_s, kvy_r,
+         g_s, g_r, o_s, o_r, dq_s, dq_r, dkvy_s, dkvy_r, dkv_s, dkv_r, b_s, b_r, by_s, by_r,
+         c_s, c_r):
     dp = lax.axis_index("dp")
     me = lax.axis_index("ctx")
     col, z = me // PLANE, lax.rem(me, PLANE)
@@ -67,7 +70,7 @@
     base = dp - part
     x, core = part // 2, lax.rem(part, 2)
     partner = base + 2 * x + 1 - core
-    ctx_peers = [lax.rem(me + i, CTX) for i in range(1, CTX)]
+    col_peers = [lax.rem(col + i, COLS) for i in range(1, COLS)]
     dp_peers = [lax.rem(dp + i, DP) for i in range(1, DP)]
     z_peers = [lax.rem(z + i, PLANE) for i in range(1, PLANE)]
     x_peers = [lax.rem(x + i, 4) for i in range(1, 4)]
@@ -87,27 +90,33 @@
     def greet(**where):
         pl.semaphore_signal(barrier, inc=1, device_id=where, device_id_type=MESH)
 
-    for peer in ctx_peers:
-        greet(ctx=peer)
+    for peer in z_peers:
+        greet(ctx=col * PLANE + peer)
+    for peer in col_peers:
+        greet(ctx=peer * PLANE + z)
     for peer in dp_peers:
         greet(dp=peer)
     for i in range(1, PLANE):
-        greet(dp=base + z, ctx=col * PLANE + lax.rem(z + i, PLANE))
-        greet(dp=base + lax.rem(part + i, PLANE), ctx=col * PLANE + part)
+        other = lax.rem(part + i, PLANE)
+        greet(dp=base + other, ctx=col * PLANE + part)
+        greet(dp=base + other, ctx=col * PLANE + lax.rem(z + PLANE - other, PLANE))
+    stays = part == 0
 
     @pl.when(jnp.logical_not(here))
     def _():
-        greet(dp=base + z, ctx=me)
         greet(dp=dp, ctx=col * PLANE + part)
+
+    @pl.when(jnp.logical_not(stays))
+    def _():
+        greet(dp=dp, ctx=col * PLANE + lax.rem(z + PLANE - part, PLANE))
 
     low16 = low_half((16, 128))
     low = low_half((BLK, 128))
     loads[0].wait()
-    pair = w_ref[:, pl.ds(pl.multiple_of(128 * (part // 2), 128), 128)]
-    odd = (lax.rem(part, 2) == 1).astype(F32)
-    tile = pair_up(pair[:16], pair[16:], 0) * (1.0 - odd) + pair_up(pair[:16], pair[16:], 1) * odd
-    w_tile[...] = tile.astype(BF16)
-    w_all[me] = tile.astype(BF16)
+    for head in range(HEADS):
+        cols = slice(128 * (head // 2), 128 * (head // 2) + 128)
+        w_tile[head] = pair_up(w_ref[:16, cols], w_ref[16:, cols], head % 2).astype(BF16)
+    w_all[me] = w_tile[lax.rem(part + z, HEADS)]
     loads[2].wait()
     for head in range(HEADS):
         cols = slice(128 * (head // 2), 128 * (head // 2) + 128)
@@ -122,31 +131,78 @@
             ).astype(BF16)
     loads[1].wait()
 
-    barrier_count = CTX - 1 + DP - 1 + 2 * (PLANE - 1) + jnp.where(here, 0, 2)
+    barrier_count = PLANE - 1 + COLS - 1 + DP - 1 + 2 * (PLANE - 1)
+    barrier_count = barrier_count + jnp.where(here, 0, 1) + jnp.where(stays, 0, 1)
     pl.semaphore_wait(barrier, barrier_count)
 
-    w_copies, og_copies, og_core, q_copies, kv_copies = [], [], [], [], []
-    for i, peer in enumerate(ctx_peers):
-        w_copies.append(remote(w_tile, w_all.at[me], w_s.at[i], w_r.at[i], ctx=peer))
+    w_copies, wy_copies, og_copies, og_core, q_copies, kv_copies, kvy_copies = [], [], [], [], [], [], []
+
+    def rank_rows(ref, rank):
+        return ref.at[pl.ds(2 * rank, 2)]
+
+    right, left = lax.rem(col + 1, COLS), lax.rem(col + COLS - 1, COLS)
+    to_right, to_left = [], []
+
+    def pass_on(rank, n, to, kept):
+        rows = rank_rows(kv_all, rank)
+        copy = remote(rows, rows, kvy_s.at[n], kvy_r.at[n], ctx=to * PLANE + z)
+        copy.start()
+        kept.append(copy)
+        kvy_copies.append(copy)
+
+    def down_column(i):
+        rank = col * PLANE + lax.rem(z + PLANE - i, PLANE)
+        pass_on(rank, 2 * i, right, to_right)
+        pass_on(rank, 2 * i + 1, left, to_left)
+
+    def across_column(i):
+        at = lax.rem(z + PLANE - i, PLANE)
+        if i % 2 == 0:
+            to_right[i].wait_recv()
+            pass_on(left * PLANE + at, 2 * PLANE + i, right, far)
+        else:
+            to_left[i].wait_recv()
+            pass_on(right * PLANE + at, 2 * PLANE + i, left, far)
+
+    far = []
+    for i, peer in enumerate(z_peers):
+        w_copies.append(
+            remote(w_tile.at[lax.rem(part + peer, HEADS)], w_all.at[me], w_s.at[i], w_r.at[i],
+                   ctx=col * PLANE + peer)
+        )
+        w_copies[i].start()
+    mine = og_all.at[part]
     for i, peer in enumerate(x_peers):
-        mine = og_all.at[part]
-        og_copies.append(
-            remote(mine, mine, og_s.at[i], og_r.at[i], dp=base + 2 * peer + core)
-        )
-    og_core.append(remote(og_all.at[part], og_all.at[part], oc_s.at[3], oc_r.at[3], dp=partner))
+        og_copies.append(remote(mine, mine, og_s.at[i], og_r.at[i], dp=base + 2 * peer + core))
+        og_copies[i].start()
+    for i, peer in enumerate(z_peers):
+        copy = remote(kv_pack.at[peer], rank_rows(kv_all, me), kv_s.at[i], kv_r.at[i],
+                      ctx=col * PLANE + peer)
+        copy.start()
+        kv_copies.append(copy)
+    kv_all[pl.ds(2 * me, 2)] = kv_pack[z]
+    down_column(0)
+    og_core.append(remote(mine, mine, oc_s.at[3], oc_r.at[3], dp=partner))
+    og_core[0].start()
+    for copy in w_copies:
+        copy.wait()
+    for j, peer in enumerate(col_peers):
+        rows = w_all.at[pl.ds(col * PLANE, PLANE)]
+        copy = remote(rows, rows, wy_s.at[j], wy_r.at[j], ctx=peer * PLANE + z)
+        copy.start()
+        wy_copies.append(copy)
     for i, peer in enumerate(z_peers):
         q_copies.append(
             remote(q_pack.at[peer], q_all.at[z], q_s.at[i], q_r.at[i], ctx=col * PLANE + peer)
         )
-    for i, peer in enumerate(ctx_peers):
-        kv_copies.append(
-            remote(kv_pack.at[lax.rem(peer, PLANE)], kv_all.at[pl.ds(2 * me, 2)],
-                   kv_s.at[i], kv_r.at[i], ctx=peer)
-        )
-    for copy in w_copies + og_copies + og_core + q_copies + kv_copies:
-        copy.start()
+        q_copies[i].start()
     q_all[z] = q_pack[z]
-    kv_all[pl.ds(2 * me, 2)] = kv_pack[z]
+
+    for i in range(1, PLANE):
+        kv_copies[i - 1].wait_recv()
+        down_column(i)
+        if i > LAG:
+            across_column(i - LAG - 1)
 
     for i in range(3):
         og_copies[i].wait_recv()
@@ -154,7 +210,9 @@
         copy = remote(og_all.at[slot], og_all.at[slot], oc_s.at[i], oc_r.at[i], dp=partner)
         copy.start()
         og_core.append(copy)
-    for copy in w_copies:
+    for i in range(PLANE - LAG - 1, PLANE):
+        across_column(i)
+    for copy in wy_copies:
         copy.wait()
     for copy in og_core:
         copy.wait_recv()
@@ -170,23 +228,26 @@
         grad = grad + pltpu.roll(grad, HEAD_DIM, 1)
         g_pack[s] = jnp.where(low, grad[:BLK], grad[BLK:]).astype(BF16)
     g_copies = []
+    head = lax.rem(part + z, HEADS)
     for i in range(PLANE):
         peer = lax.rem(part + i, PLANE)
         copy = remote(g_pack.at[peer], g_all.at[z], g_s.at[i], g_r.at[z],
-                      dp=base + peer, ctx=col * PLANE + part)
+                      dp=base + peer, ctx=col * PLANE + head)
         g_copies.append(copy)
         if i:
             copy.start()
         else:
-            pl.when(jnp.logical_not(here))(copy.start)
-
-            @pl.when(here)
+            pl.when(jnp.logical_not(stays))(copy.start)
+
+            @pl.when(stays)
             def _():
                 g_all[z] = g_pack[part]
 
     for s in range(PLANE):
         og_t[:, 128 * s:128 * s + 128] = og_all[s].T
-    for copy in q_copies + kv_copies:
+    for i in range(PLANE):
+        (to_left if i % 2 == 0 else to_right)[i].wait_recv()
+    for copy in q_copies + far:
         copy.wait_recv()
 
     length = tab[T_LENGTH]
@@ -224,7 +285,7 @@
         o_pack[zp] = pair_up(outs[0], outs[1], 1).astype(BF16)
         return carry
 
-    lax.fori_loop(0, PLANE, forward, 0)
+    lax.fori_loop(0, PLANE, forward, 0, unroll=2)
 
     o_copies = []
     for i in range(PLANE):
@@ -248,7 +309,7 @@
         slot = lax.rem(z + i, PLANE)
         arrived(g_all.at[slot], g_r.at[slot])
 
-    @pl.when(jnp.logical_not(here))
+    @pl.when(jnp.logical_not(stays))
     def _():
         arrived(g_all.at[z], g_r.at[z])
 
@@ -279,7 +340,7 @@
         dq_pack[zp] = pair_up(outs[0], outs[1], 0).astype(BF16)
         return carry
 
-    lax.fori_loop(0, PLANE, backward, 0)
+    lax.fori_loop(0, PLANE, backward, 0, unroll=2)
 
     dq_copies = []
     for i, peer in enumerate(z_peers):
@@ -287,6 +348,34 @@
         copy.start()
         dq_copies.append(copy)
     dq_all[z] = dq_pack[z]
+
+    sums[ENTRIES] = jnp.zeros((BLK, 128), F32)
+
+    def accumulate(t, total):
+        total = entry_grads[tab[T_PERM + t]] + total * tab[T_SAME + t].astype(F32)
+        sums[t] = total
+        return total
+
+    lax.fori_loop(0, ENTRIES, accumulate, jnp.zeros((BLK, 128), F32), unroll=4)
+
+    def pack(c, carry):
+        for half in range(2):
+            dkv_pack[c, half] = sums[tab[T_LAST + 2 * c + half]].astype(BF16)
+        return carry
+
+    lax.fori_loop(0, CTX, pack, 0, unroll=2)
+    dkvy_copies, dkv_copies = [], []
+
+    def send_dkv(i):
+        zc = lax.rem(z + 1 + i, PLANE)
+        for j, peer in enumerate(col_peers):
+            copy = remote(dkv_pack.at[peer * PLANE + zc], dkv_y.at[j, zc], dkvy_s.at[3 * i + j],
+                          dkvy_r.at[3 * i + j], ctx=peer * PLANE + z)
+            copy.start()
+            dkvy_copies.append(copy)
+
+    for i in range(2):
+        send_dkv(i)
 
     for i in range(1, PLANE):
         slot = lax.rem(part + i, PLANE)
@@ -306,45 +395,49 @@
         grad = dot(og_t[32 * c:32 * c + 256], attention)
         grad = ((grad + pltpu.roll(grad, HEAD_DIM, 1)) * WG_SCALE).reshape(8, 2, 16, 128)
         for k in range(8):
-            wg_pack[c + k] = jnp.where(low16, grad[k, 0], grad[k, 1]).astype(BF16)
-    b_copies = []
-    for i, peer in enumerate(ctx_peers):
-        copy = remote(wg_pack.at[peer], wg_in.at[me], b_s.at[i], b_r.at[i], ctx=peer)
+            wg_pack[c // PLANE, k] = jnp.where(low16, grad[k, 0], grad[k, 1]).astype(BF16)
+    by_copies, b_copies, c_copies = [], [], []
+    for j, peer in enumerate(col_peers):
+        copy = remote(wg_pack.at[peer], wg_in.at[col], by_s.at[j], by_r.at[j], ctx=peer * PLANE + z)
+        copy.start()
+        by_copies.append(copy)
+    wg_in[col] = wg_pack[col]
+
+    for i in range(2, PLANE):
+        send_dkv(i)
+
+    for copy in by_copies:
+        copy.wait()
+    wg_mid[...] = sum(wg_in[i].astype(F32) for i in range(COLS)).astype(BF16)
+    for i, peer in enumerate(z_peers):
+        copy = remote(wg_mid.at[peer], wg_col.at[z], b_s.at[i], b_r.at[i], ctx=col * PLANE + peer)
         copy.start()
         b_copies.append(copy)
-    wg_in[me] = wg_pack[me]
-
-    sums[ENTRIES] = jnp.zeros((BLK, 128), F32)
-
-    def accumulate(t, total):
-        total = entry_grads[tab[T_PERM + t]] + total * tab[T_SAME + t].astype(F32)
-        sums[t] = total
-        return total
-
-    lax.fori_loop(0, ENTRIES, accumulate, jnp.zeros((BLK, 128), F32), unroll=4)
-
-    def pack(c, carry):
-        for half in range(2):
-            dkv_pack[c, half] = sums[tab[T_LAST + 2 * c + half]].astype(BF16)
-        return carry
-
-    lax.fori_loop(0, CTX, pack, 0, unroll=2)
-    dkv_copies = []
-    for i, peer in enumerate(ctx_peers):
-        copy = remote(dkv_pack.at[peer], dkv_in.at[me], dkv_s.at[i], dkv_r.at[i], ctx=peer)
-        copy.start()
-        dkv_copies.append(copy)
-    dkv_in[me] = dkv_pack[me]
-
-    for copy in b_copies:
-        copy.wait()
-    wg_last[...] = sum(wg_in[i].astype(F32) for i in range(CTX)).astype(BF16)
-    c_copies = []
-    for i, peer in enumerate(dp_peers):
-        copy = remote(wg_last, wg_all.at[dp], c_s.at[i], c_r.at[i], dp=peer)
-        copy.start()
-        c_copies.append(copy)
-    wg_all[dp] = wg_last[...]
+    wg_col[z] = wg_mid[z]
+
+    for i in range(PLANE):
+        zc = lax.rem(z + 1 + i, PLANE)
+        for j in range(COLS - 1):
+            dkvy_copies[3 * i + j].wait_recv()
+        total = dkv_pack[col * PLANE + zc].astype(F32)
+        for j in range(COLS - 1):
+            total = total + dkv_y[j, zc].astype(F32)
+        if i == PLANE - 1:
+            dkv_in[z] = total.astype(BF16)
+        else:
+            dkv_z[i] = total.astype(BF16)
+            copy = remote(dkv_z.at[i], dkv_in.at[z], dkv_s.at[i], dkv_r.at[i], ctx=col * PLANE + zc)
+            copy.start()
+            dkv_copies.append(copy)
+        if i == 1:
+            for copy in b_copies:
+                copy.wait()
+            wg_last[...] = sum(wg_col[k].astype(F32) for k in range(PLANE)).astype(BF16)
+            for k, peer in enumerate(dp_peers):
+                copy = remote(wg_last, wg_all.at[dp], c_s.at[k], c_r.at[k], dp=peer)
+                copy.start()
+                c_copies.append(copy)
+            wg_all[dp] = wg_last[...]
 
     for copy in dq_copies:
         copy.wait()
@@ -367,20 +460,21 @@
     for c in range(4):
         for half in range(2):
             rows = slice(BLK * half, BLK * half + BLK)
-            even, odd_ = [
-                sum(dkv_in[y * PLANE + head, half].astype(F32) for y in range(CTX // PLANE))
-                for head in (2 * c, 2 * c + 1)
-            ]
+            even, odd_ = dkv_in[2 * c, half], dkv_in[2 * c + 1, half]
             dkv_out[rows, 128 * c:128 * c + 128] = pair_up(even, odd_, 0).astype(BF16)
             dkv_out[rows, 512 + 128 * c:640 + 128 * c] = pair_up(even, odd_, 1).astype(BF16)
 
-    for copy in og_copies + og_core + q_copies + kv_copies + g_copies[1:] + o_copies[1:]:
+    for copy in (og_copies + og_core + q_copies + kv_copies + kvy_copies + dkvy_copies
+                 + g_copies[1:] + o_copies[1:]):
         copy.wait_send()
 
     @pl.when(jnp.logical_not(here))
     def _():
+        o_copies[0].wait_send()
+
+    @pl.when(jnp.logical_not(stays))
+    def _():
         g_copies[0].wait_send()
-        o_copies[0].wait_send()
 
 
 def table(block_list, counts, length, first):
@@ -406,8 +500,9 @@
     tab = table(block_lists[0], block_counts[0], seq_lengths, first)
     dma = pltpu.SemaphoreType.DMA
     vm = pltpu.VMEM
-    any_space = pl.BlockSpec(memory_space=pl.ANY)
-    pairs = [CTX - 1, 3, 4, PLANE - 1, CTX - 1, PLANE, PLANE, PLANE - 1, CTX - 1, CTX - 1, DP - 1]
+    hbm = pl.BlockSpec(memory_space=pltpu.HBM)
+    zs, ys = PLANE - 1, COLS - 1
+    pairs = [zs, ys, 3, 4, zs, zs, PLANE * ys, PLANE, PLANE, zs, PLANE * ys, zs, zs, ys, DP - 1]
     return pl.pallas_call(
         body,
         out_shape=(
@@ -415,11 +510,11 @@
             jax.ShapeDtypeStruct((128, 1024), BF16),
             jax.ShapeDtypeStruct((32, 512), F32),
         ),
-        in_specs=[pl.BlockSpec(memory_space=pltpu.SMEM)] + [any_space] * 4,
+        in_specs=[pl.BlockSpec(memory_space=pltpu.SMEM)] + [hbm] * 4,
         out_specs=tuple([pl.BlockSpec(memory_space=pltpu.VMEM)] * 3),
         scratch_shapes=[
             vm((128, 512), BF16), vm((128, 1024), BF16), vm((32, 512), BF16),
-            vm((16, 128), BF16), vm((CTX, 16, 128), BF16),
+            vm((HEADS, 16, 128), BF16), vm((CTX, 16, 128), BF16),
             vm((PLANE, 128, 1024), BF16), vm((1024, 1024), BF16),
             vm((HEADS, BLK, 128), BF16), vm((PLANE, BLK, 128), BF16),
             vm((HEADS, 2, BLK, 128), BF16), vm((NQB, BLK, 128), BF16),
@@ -428,13 +523,15 @@
             vm((PLANE, BLK, 128), BF16), vm((PLANE, BLK, 128), BF16),
             vm((PLANE, BLK, 128), BF16), vm((PLANE, BLK, 128), BF16),
             vm((ENTRIES, BLK, 128), F32), vm((ENTRIES + 1, BLK, 128), F32),
-            vm((CTX, 2, BLK, 128), BF16), vm((CTX, 2, BLK, 128), BF16),
-            vm((CTX, 16, 128), BF16), vm((CTX, 16, 128), BF16),
+            vm((CTX, 2, BLK, 128), BF16), vm((COLS - 1, PLANE, 2, BLK, 128), BF16),
+            vm((PLANE - 1, 2, BLK, 128), BF16), vm((HEADS, 2, BLK, 128), BF16),
+            vm((COLS, PLANE, 16, 128), BF16), vm((COLS, PLANE, 16, 128), BF16),
+            vm((PLANE, 16, 128), BF16), vm((PLANE, 16, 128), BF16),
             vm((16, 128), BF16), vm((DP, 16, 128), BF16),
             dma((4,)),
         ] + [dma((n,)) for n in pairs for _ in range(2)],
         compiler_params=pltpu.CompilerParams(
-            collective_id=0, has_side_effects=True, vmem_limit_bytes=48 * 2**20
+            collective_id=0, has_side_effects=True, vmem_limit_bytes=60 * 2**20
         ),
         name="attention_step",
     )(tab, queries, keyvals, out_weight, out_grad)

time: 118 us -> 99.3 us (0.84)
  Pallas kernels: 111 us -> 92.3 us
    pallas_call x1, Pallas kernels: 111 us -> 92.3 us  [per_device(): pl.pallas_call(body, out_shape=(jax.ShapeDtypeStruct((128, 512), BF16), j...]
    unnamed x15 -> x11, local copies, waits for them, and re-layouts: 4.81 us -> 3.12 us
where the time goes in v3:
time: 99.3 us; the launch traced here: 98.2 us
  Pallas kernels  92.3 us (93%)
  local copies, waits for them, and re-layouts  4.09 us (4%)
  between operations  1.38 us (1%)
    pallas_call x1, Pallas kernels, per_device(): pl.pallas_call(body, out_shape=(jax.ShapeDtypeStruct((128, 512), BF16), j...  92.3 us
    unnamed x11, local copies, waits for them, and re-layouts  3.12 us

profile of v3, /device:TPU:1, one launch (start us, length us, event | category | flops | bytes accessed | tf_op | source)
XLA Modules:
  0.0 98.2 jit_solution(10940465125554972401)
XLA Ops:
  0.6 0.0 copy-start
  0.7 0.0 copy-start.3
  1.3 0.0 copy-done.3
  1.3 0.1 dynamic-slice_bitcast_fusion
  1.4 0.0 copy-done
  1.4 0.1 constant_dynamic-slice_fusion
  1.5 0.1 copy.12
  1.6 0.1 reshape.36
  1.7 0.2 convert_reduce_fusion
  1.9 0.1 select_reduce_fusion
  2.0 0.1 convert_reduce_fusion.2
  2.1 0.7 concatenate.3.tab
  2.8 92.3 %attention_step.1 = (bf16[128,512]{1,0:T(8,128)(2,1)}, bf16[128,1024]{1,0:T(8,128)(2,1)}, f32[32,512]{1,0:T(8,128)}) custom-call(s32[465]{0:T(512)} %concatenate.3.tab, bf16[128,512]{1,0:T(8,128)(2,1)} %q_hbm.1, bf16[128,1024]{1,0:T(8,128)(2,1)} %kv_hbm.1, bf16[32,512]{1,0:T(8,128)(2,1)} %w_hbm.1, bf16[128,1024]{1,0:T(8,128)(2,1)} %og_hbm.1), custom_call_target="tpu_custom_call" | custom-call | tf_op jit(solution)/shard_map/attention_step/pallas_call | solution.py:506
  95.1 0.0 copy-start.1
  95.1 1.6 %copy.17 = bf16[128,512]{1,0:T(8,128)(2,1)} copy(bf16[128,512]{1,0:T(8,128)(2,1)} %get-tuple-element.12) | data formatting | bytes 262144
  96.7 0.0 copy-done.1
  96.7 0.0 copy-start.2
  96.7 0.7 copy.18
  97.4 0.2 copy-done.2
  97.6 0.6 copy.19
  (2 shorter events, 0.0 us)
Async XLA Ops:
  0.6 0.8 copy-start
  0.7 0.7 copy-start.3
  95.1 1.6 %copy-start.1 = (bf16[128,1024]{1,0:T(8,128)(2,1)S(1)}, bf16[128,1024]{1,0:T(8,128)(2,1)}, u32[]{:S(2)}) copy-start(bf16[128,1024]{1,0:T(8,128)(2,1)} %get-tuple-element.13) | copy-start | bytes 786436
  96.7 0.9 copy-start.2

commit v4 on v3

--- a/solution.py
+++ b/solution.py
@@ -59,7 +59,7 @@
 def body(tab, q_hbm, kv_hbm, w_hbm, og_hbm, dq_out, dkv_out, wg_out,
          q_ref, kv_ref, w_ref, w_tile, w_all, og_all, og_t, q_pack, q_all, kv_pack, kv_all,
          g_pack, g_all, p_all, o_pack, o_all, dq_pack, dq_all, entry_grads, sums,
-         dkv_pack, dkv_y, dkv_z, dkv_in, wg_pack, wg_in, wg_mid, wg_col, wg_last, wg_all,
+         dkv_pack, dkv_y, dkv_mix, dkv_z, dkv_in, wg_pack, wg_in, wg_mid, wg_col, wg_last, wg_all,
          in_sem, w_s, w_r, wy_s, wy_r, og_s, og_r, oc_s, oc_r, q_s, q_r, kv_s, kv_r, kvy_s, kvy_r,
          g_s, g_r, o_s, o_r, dq_s, dq_r, dkvy_s, dkvy_r, dkv_s, dkv_r, b_s, b_r, by_s, by_r,
          c_s, c_r):
@@ -210,8 +210,6 @@
         copy = remote(og_all.at[slot], og_all.at[slot], oc_s.at[i], oc_r.at[i], dp=partner)
         copy.start()
         og_core.append(copy)
-    for i in range(PLANE - LAG - 1, PLANE):
-        across_column(i)
     for copy in wy_copies:
         copy.wait()
     for copy in og_core:
@@ -243,6 +241,8 @@
             def _():
                 g_all[z] = g_pack[part]
 
+    for i in range(PLANE - LAG - 1, PLANE):
+        across_column(i)
     for s in range(PLANE):
         og_t[:, 128 * s:128 * s + 128] = og_all[s].T
     for i in range(PLANE):
@@ -366,13 +366,29 @@
     lax.fori_loop(0, CTX, pack, 0, unroll=2)
     dkvy_copies, dkv_copies = [], []
 
+    opposite = lax.rem(col + 2, COLS)
+    far_copies, mixed_copies = [], []
+
+    def step_dkv(i, n, src, slot, to):
+        zc = lax.rem(z + 1 + i, PLANE)
+        copy = remote(src, dkv_y.at[slot, zc], dkvy_s.at[3 * i + n], dkvy_r.at[3 * i + n],
+                      ctx=to * PLANE + z)
+        copy.start()
+        return copy
+
     def send_dkv(i):
         zc = lax.rem(z + 1 + i, PLANE)
-        for j, peer in enumerate(col_peers):
-            copy = remote(dkv_pack.at[peer * PLANE + zc], dkv_y.at[j, zc], dkvy_s.at[3 * i + j],
-                          dkvy_r.at[3 * i + j], ctx=peer * PLANE + z)
-            copy.start()
-            dkvy_copies.append(copy)
+        ahead, behind = (right, left) if i % 2 == 0 else (left, right)
+        far_copies.append(step_dkv(i, 0, dkv_pack.at[opposite * PLANE + zc], 2, ahead))
+        dkvy_copies.append(step_dkv(i, 1, dkv_pack.at[behind * PLANE + zc], 0, behind))
+
+    def mix_dkv(i):
+        zc = lax.rem(z + 1 + i, PLANE)
+        ahead = right if i % 2 == 0 else left
+        far_copies[i].wait_recv()
+        total = dkv_pack[ahead * PLANE + zc].astype(F32) + dkv_y[2, zc].astype(F32)
+        dkv_mix[i] = total.astype(BF16)
+        mixed_copies.append(step_dkv(i, 2, dkv_mix.at[i], 1, ahead))
 
     for i in range(2):
         send_dkv(i)
@@ -405,6 +421,7 @@
 
     for i in range(2, PLANE):
         send_dkv(i)
+        mix_dkv(i - 2)
 
     for copy in by_copies:
         copy.wait()
@@ -417,10 +434,12 @@
 
     for i in range(PLANE):
         zc = lax.rem(z + 1 + i, PLANE)
-        for j in range(COLS - 1):
-            dkvy_copies[3 * i + j].wait_recv()
+        if i < 2:
+            mix_dkv(PLANE - 2 + i)
+        dkvy_copies[i].wait_recv()
+        mixed_copies[i].wait_recv()
         total = dkv_pack[col * PLANE + zc].astype(F32)
-        for j in range(COLS - 1):
+        for j in range(2):
             total = total + dkv_y[j, zc].astype(F32)
         if i == PLANE - 1:
             dkv_in[z] = total.astype(BF16)
@@ -464,8 +483,8 @@
             dkv_out[rows, 128 * c:128 * c + 128] = pair_up(even, odd_, 0).astype(BF16)
             dkv_out[rows, 512 + 128 * c:640 + 128 * c] = pair_up(even, odd_, 1).astype(BF16)
 
-    for copy in (og_copies + og_core + q_copies + kv_copies + kvy_copies + dkvy_copies
-                 + g_copies[1:] + o_copies[1:]):
+    for copy in (og_copies + og_core + q_copies + kv_copies + kvy_copies + dkvy_copies + far_copies
+                 + mixed_copies + g_copies[1:] + o_copies[1:]):
         copy.wait_send()
 
     @pl.when(jnp.logical_not(here))
@@ -524,7 +543,8 @@
             vm((PLANE, BLK, 128), BF16), vm((PLANE, BLK, 128), BF16),
             vm((ENTRIES, BLK, 128), F32), vm((ENTRIES + 1, BLK, 128), F32),
             vm((CTX, 2, BLK, 128), BF16), vm((COLS - 1, PLANE, 2, BLK, 128), BF16),
-            vm((PLANE - 1, 2, BLK, 128), BF16), vm((HEADS, 2, BLK, 128), BF16),
+            vm((PLANE, 2, BLK, 128), BF16), vm((PLANE - 1, 2, BLK, 128), BF16),
+            vm((HEADS, 2, BLK, 128), BF16),
             vm((COLS, PLANE, 16, 128), BF16), vm((COLS, PLANE, 16, 128), BF16),
             vm((PLANE, 16, 128), BF16), vm((PLANE, 16, 128), BF16),
             vm((16, 128), BF16), vm((DP, 16, 128), BF16),

time: 99.3 us -> 93.9 us (0.946)
  the two profiles are of different devices: /device:TPU:1 before, /device:TPU:16 now
where the time goes in v4:
time: 93.9 us; the launch traced here: 93.7 us
  Pallas kernels  87.8 us (94%)
  local copies, waits for them, and re-layouts  4.09 us (4%)
  between operations  1.38 us (1%)
    pallas_call x1, Pallas kernels, per_device(): pl.pallas_call(body, out_shape=(jax.ShapeDtypeStruct((128, 512), BF16), j...  87.8 us
    unnamed x11, local copies, waits for them, and re-layouts  3.12 us

profile of v4, /device:TPU:16, one launch (start us, length us, event | category | flops | bytes accessed | tf_op | source)
XLA Modules:
  0.0 93.7 jit_solution(17566817213246244971)
XLA Ops:
  0.6 0.0 copy-start
  0.7 0.0 copy-start.3
  1.3 0.0 copy-done.3
  1.3 0.1 dynamic-slice_bitcast_fusion
  1.4 0.0 copy-done
  1.4 0.1 constant_dynamic-slice_fusion
  1.5 0.1 copy.12
  1.6 0.1 reshape.36
  1.7 0.2 convert_reduce_fusion
  1.9 0.1 select_reduce_fusion
  2.0 0.1 convert_reduce_fusion.2
  2.1 0.7 concatenate.3.tab
  2.8 87.8 %attention_step.1 = (bf16[128,512]{1,0:T(8,128)(2,1)}, bf16[128,1024]{1,0:T(8,128)(2,1)}, f32[32,512]{1,0:T(8,128)}) custom-call(s32[465]{0:T(512)} %concatenate.3.tab, bf16[128,512]{1,0:T(8,128)(2,1)} %q_hbm.1, bf16[128,1024]{1,0:T(8,128)(2,1)} %kv_hbm.1, bf16[32,512]{1,0:T(8,128)(2,1)} %w_hbm.1, bf16[128,1024]{1,0:T(8,128)(2,1)} %og_hbm.1), custom_call_target="tpu_custom_call" | custom-call | tf_op jit(solution)/shard_map/attention_step/pallas_call | solution.py:525
  90.6 0.0 copy-start.1
  90.6 1.6 %copy.17 = bf16[128,512]{1,0:T(8,128)(2,1)} copy(bf16[128,512]{1,0:T(8,128)(2,1)} %get-tuple-element.12) | data formatting | bytes 262144
  92.2 0.0 copy-done.1
  92.2 0.0 copy-start.2
  92.2 0.7 copy.18
  92.9 0.2 copy-done.2
  93.0 0.6 copy.19
  (2 shorter events, 0.0 us)
Async XLA Ops:
  0.6 0.8 copy-start
  0.7 0.7 copy-start.3
  90.6 1.6 %copy-start.1 = (bf16[128,1024]{1,0:T(8,128)(2,1)S(1)}, bf16[128,1024]{1,0:T(8,128)(2,1)}, u32[]{:S(2)}) copy-start(bf16[128,1024]{1,0:T(8,128)(2,1)} %get-tuple-element.13) | copy-start | bytes 786436
  92.2 0.9 copy-start.2

commit v5 on v4

--- a/solution.py
+++ b/solution.py
@@ -14,7 +14,7 @@
 NQB = 64
 CTX = 32
 COLS = 4
-LAG = 2
+LAG = 3
 DP = 16
 PLANE = 8
 UNITS = 16
@@ -356,14 +356,12 @@
         sums[t] = total
         return total
 
-    lax.fori_loop(0, ENTRIES, accumulate, jnp.zeros((BLK, 128), F32), unroll=4)
-
-    def pack(c, carry):
+    lax.fori_loop(0, ENTRIES, accumulate, jnp.zeros((BLK, 128), F32), unroll=16)
+
+    def pack(c):
         for half in range(2):
             dkv_pack[c, half] = sums[tab[T_LAST + 2 * c + half]].astype(BF16)
-        return carry
-
-    lax.fori_loop(0, CTX, pack, 0, unroll=2)
+
     dkvy_copies, dkv_copies = [], []
 
     opposite = lax.rem(col + 2, COLS)
@@ -379,6 +377,8 @@
     def send_dkv(i):
         zc = lax.rem(z + 1 + i, PLANE)
         ahead, behind = (right, left) if i % 2 == 0 else (left, right)
+        for y in (opposite, behind, ahead):
+            pack(y * PLANE + zc)
         far_copies.append(step_dkv(i, 0, dkv_pack.at[opposite * PLANE + zc], 2, ahead))
         dkvy_copies.append(step_dkv(i, 1, dkv_pack.at[behind * PLANE + zc], 0, behind))
 
@@ -434,6 +434,7 @@
 
     for i in range(PLANE):
         zc = lax.rem(z + 1 + i, PLANE)
+        pack(col * PLANE + zc)
         if i < 2:
             mix_dkv(PLANE - 2 + i)
         dkvy_copies[i].wait_recv()

time: 93.9 us -> 92.4 us (0.984)
  the two profiles are of different devices: /device:TPU:16 before, /device:TPU:1 now
where the time goes in v5:
time: 92.4 us; the launch traced here: 92.2 us
  Pallas kernels  86.3 us (93%)
  local copies, waits for them, and re-layouts  4.09 us (4%)
  between operations  1.38 us (1%)
    pallas_call x1, Pallas kernels, per_device(): pl.pallas_call(body, out_shape=(jax.ShapeDtypeStruct((128, 512), BF16), j...  86.3 us
    unnamed x11, local copies, waits for them, and re-layouts  3.12 us

profile of v5, /device:TPU:1, one launch (start us, length us, event | category | flops | bytes accessed | tf_op | source)
XLA Modules:
  0.0 92.2 jit_solution(10013229426223136738)
XLA Ops:
  0.6 0.0 copy-start
  0.7 0.0 copy-start.3
  1.3 0.0 copy-done.3
  1.3 0.1 dynamic-slice_bitcast_fusion
  1.4 0.0 copy-done
  1.4 0.1 constant_dynamic-slice_fusion
  1.5 0.1 copy.12
  1.6 0.1 reshape.36
  1.7 0.2 convert_reduce_fusion
  1.9 0.1 select_reduce_fusion
  2.0 0.1 convert_reduce_fusion.2
  2.1 0.7 concatenate.3.tab
  2.8 86.3 %attention_step.1 = (bf16[128,512]{1,0:T(8,128)(2,1)}, bf16[128,1024]{1,0:T(8,128)(2,1)}, f32[32,512]{1,0:T(8,128)}) custom-call(s32[465]{0:T(512)} %concatenate.3.tab, bf16[128,512]{1,0:T(8,128)(2,1)} %q_hbm.1, bf16[128,1024]{1,0:T(8,128)(2,1)} %kv_hbm.1, bf16[32,512]{1,0:T(8,128)(2,1)} %w_hbm.1, bf16[128,1024]{1,0:T(8,128)(2,1)} %og_hbm.1), custom_call_target="tpu_custom_call" | custom-call | tf_op jit(solution)/shard_map/attention_step/pallas_call | solution.py:526
  89.1 0.0 copy-start.1
  89.1 1.6 %copy.17 = bf16[128,512]{1,0:T(8,128)(2,1)} copy(bf16[128,512]{1,0:T(8,128)(2,1)} %get-tuple-element.12) | data formatting | bytes 262144
  90.7 0.0 copy-done.1
  90.7 0.0 copy-start.2
  90.7 0.7 copy.18
  91.4 0.2 copy-done.2
  91.6 0.6 copy.19
  (2 shorter events, 0.0 us)
Async XLA Ops:
  0.6 0.8 copy-start
  0.7 0.7 copy-start.3
  89.1 1.6 %copy-start.1 = (bf16[128,1024]{1,0:T(8,128)(2,1)S(1)}, bf16[128,1024]{1,0:T(8,128)(2,1)}, u32[]{:S(2)}) copy-start(bf16[128,1024]{1,0:T(8,128)(2,1)} %get-tuple-element.13) | copy-start | bytes 786436
  90.7 0.9 copy-start.2

commit v6 on v5

--- a/solution.py
+++ b/solution.py
@@ -285,7 +285,7 @@
         o_pack[zp] = pair_up(outs[0], outs[1], 1).astype(BF16)
         return carry
 
-    lax.fori_loop(0, PLANE, forward, 0, unroll=2)
+    lax.fori_loop(0, PLANE, forward, 0, unroll=4)
 
     o_copies = []
     for i in range(PLANE):
@@ -340,7 +340,7 @@
         dq_pack[zp] = pair_up(outs[0], outs[1], 0).astype(BF16)
         return carry
 
-    lax.fori_loop(0, PLANE, backward, 0, unroll=2)
+    lax.fori_loop(0, PLANE, backward, 0, unroll=4)
 
     dq_copies = []
     for i, peer in enumerate(z_peers):

time: 92.4 us -> 91.4 us (0.989)
  Pallas kernels: 86.3 us -> 84.6 us
    pallas_call x1, Pallas kernels: 86.3 us -> 84.6 us  [per_device(): pl.pallas_call(body, out_shape=(jax.ShapeDtypeStruct((128, 512), BF16), j...]
where the time goes in v6:
time: 91.4 us; the launch traced here: 90.5 us
  Pallas kernels  84.6 us (93%)
  local copies, waits for them, and re-layouts  4.09 us (4%)
  between operations  1.38 us (2%)
    pallas_call x1, Pallas kernels, per_device(): pl.pallas_call(body, out_shape=(jax.ShapeDtypeStruct((128, 512), BF16), j...  84.6 us
    unnamed x11, local copies, waits for them, and re-layouts  3.12 us

profile of v6, /device:TPU:1, one launch (start us, length us, event | category | flops | bytes accessed | tf_op | source)
XLA Modules:
  0.0 90.5 jit_solution(773654295036313017)
XLA Ops:
  0.6 0.0 copy-start
  0.7 0.0 copy-start.3
  1.3 0.0 copy-done.3
  1.3 0.1 dynamic-slice_bitcast_fusion
  1.4 0.0 copy-done
  1.4 0.1 constant_dynamic-slice_fusion
  1.5 0.1 copy.12
  1.6 0.1 reshape.36
  1.7 0.2 convert_reduce_fusion
  1.9 0.1 select_reduce_fusion
  2.0 0.1 convert_reduce_fusion.2
  2.1 0.7 concatenate.3.tab
  2.8 84.6 %attention_step.1 = (bf16[128,512]{1,0:T(8,128)(2,1)}, bf16[128,1024]{1,0:T(8,128)(2,1)}, f32[32,512]{1,0:T(8,128)}) custom-call(s32[465]{0:T(512)} %concatenate.3.tab, bf16[128,512]{1,0:T(8,128)(2,1)} %q_hbm.1, bf16[128,1024]{1,0:T(8,128)(2,1)} %kv_hbm.1, bf16[32,512]{1,0:T(8,128)(2,1)} %w_hbm.1, bf16[128,1024]{1,0:T(8,128)(2,1)} %og_hbm.1), custom_call_target="tpu_custom_call" | custom-call | tf_op jit(solution)/shard_map/attention_step/pallas_call | solution.py:526
  87.4 0.0 copy-start.1
  87.4 1.6 %copy.17 = bf16[128,512]{1,0:T(8,128)(2,1)} copy(bf16[128,512]{1,0:T(8,128)(2,1)} %get-tuple-element.12) | data formatting | bytes 262144
  89.0 0.0 copy-done.1
  89.0 0.0 copy-start.2
  89.0 0.7 copy.18
  89.7 0.2 copy-done.2
  89.9 0.6 copy.19
  (2 shorter events, 0.0 us)
Async XLA Ops:
  0.6 0.8 copy-start
  0.7 0.7 copy-start.3
  87.4 1.6 %copy-start.1 = (bf16[128,1024]{1,0:T(8,128)(2,1)S(1)}, bf16[128,1024]{1,0:T(8,128)(2,1)}, u32[]{:S(2)}) copy-start(bf16[128,1024]{1,0:T(8,128)(2,1)} %get-tuple-element.13) | copy-start | bytes 786436
  89.0 0.9 copy-start.2
